TPU v7x, 128 devices: a whole 4x4x4 slice. The times are simulated.
128 devices in a mesh: gx: 4 (over y), gy: 4 (over z), gz: 8 (over x, core).
Axes of the slice: x: 4, y: 4, z: 4, core: 2. Of those that a mesh axis runs over, the one named last changes fastest.
Arguments:
- points: float32 [262144, 512], P(('gx', 'gy', 'gz')), may hold values from -6 to 6
- order: int32 [262144], P(('gx', 'gy', 'gz')), may hold values from 0 to 262143, as said below
- near: bfloat16 [256, 1024, 1024], P(('gx', 'gy', 'gz')), may hold values from -0.1875 to 0.1875
- basis_in: bfloat16 [256, 1024, 256], P(('gx', 'gy', 'gz')), may hold values from -0.1875 to 0.1875
- basis_out: bfloat16 [256, 1024, 256], P(('gx', 'gy', 'gz')), may hold values from -0.375 to 0.375
- leaf_coupling: bfloat16 [256, 3, 256, 256], P(('gx', 'gy', 'gz')), may hold values from -0.375 to 0.375
- transfer_up: bfloat16 [128, 3, 1024, 256], P(('gx', 'gy', 'gz')), may hold values from -0.09375 to 0.09375, as said below
- transfer_down: bfloat16 [128, 3, 1024, 256], P(('gx', 'gy', 'gz')), may hold values from -0.1875 to 0.1875, as said below
- node_coupling: bfloat16 [128, 3, 3, 256, 256], P(('gx', 'gy', 'gz')), may hold values from -0.1875 to 0.1875, as said below
- ridge: float32 [1], replicated, may hold values from 0.5 to 2
Outputs:
- result: float32 [262144, 512], P(('gx', 'gy', 'gz'))
Inputs may be any that keep to these rules, and one draw needn't show every extreme that they name: `order`: each device's 2048 consecutive entries are a permutation of the initial indices of those same rows. `transfer_up`: rows d and e are equal at level k whenever devices d and e have the same ancestor at level k. `transfer_down`: rows d and e are equal at level k whenever devices d and e have the same ancestor at level k. `node_coupling`: rows d and e are equal at level k whenever devices d and e have the same ancestor at level k.
All inputs are finite; a program needn't handle non-finite values.
Results may differ from a plain program's by a relative error of at most 0.014.
Values may be sent and summed in bfloat16 or wider, within the bound.
A program may use at most 128 MiB of HBM per device.

v0:
```python
import jax
import jax.numpy as jnp
import numpy as np
from jax import lax
from jax.sharding import PartitionSpec as P

SIBLINGS = np.array([[1, 2, 3], [0, 2, 3], [0, 1, 3], [0, 1, 2]], dtype=np.int32)


def from_partner(value, axis, bit):
    mask = 2**bit
    pairs = [(source, source ^ mask) for source in range(lax.axis_size(axis))]
    return lax.ppermute(value, axis, pairs)


def pair_up(node_rows, bit_place, own_index):
    partner = from_partner(node_rows, "gz", bit_place)
    is_upper = own_index >> bit_place & 1 == 1
    first_half = jnp.where(is_upper, partner, node_rows)
    second_half = jnp.where(is_upper, node_rows, partner)
    return jnp.concatenate([first_half, second_half], axis=0)


def couple_one(children, position, coupling):
    others = jnp.take(children, jnp.asarray(SIBLINGS)[position], axis=0)
    return jnp.einsum("jrs,jsc->rc", coupling, others, preferred_element_type=jnp.float32)


def lift(lifter, children):
    stacked = children.reshape(-1, children.shape[-1])
    return jnp.einsum("kr,kc->rc", lifter, stacked, preferred_element_type=jnp.float32).astype(
        jnp.bfloat16
    )


def on_device(
    points,
    order,
    near,
    basis_in,
    basis_out,
    leaf_coupling,
    transfer_up,
    transfer_down,
    node_coupling,
    ridge,
):
    rows_here = points.shape[0]
    leaf_count = near.shape[0]
    leaf_rows = near.shape[1]
    columns = points.shape[1]
    rank_size = basis_in.shape[2]
    middle = transfer_up.shape[1] - 1
    local_rows = jnp.remainder(order, rows_here)
    ordered = jnp.take(points, local_rows, axis=0)
    rounded = ordered.astype(jnp.bfloat16).reshape(leaf_count, leaf_rows, columns)
    leaf_hat = jnp.einsum(
        "nlr,nlc->nrc", basis_in, rounded, preferred_element_type=jnp.float32
    ).astype(jnp.bfloat16)
    gz_index = lax.axis_index("gz")
    gy_index = lax.axis_index("gy")
    gx_index = lax.axis_index("gx")
    children = pair_up(leaf_hat, 0, gz_index)
    node_hat = lift(transfer_up[0, 0], children)
    height = 2
    paired = pair_up(node_hat[None], 2 * height - 3, gz_index)
    level_group = pair_up(paired, 2 * height - 2, gz_index)
    slot_index = gz_index >> 2 * height - 3 & 3
    far_mid = [couple_one(level_group, slot_index, node_coupling[0, height - 2])]
    node_hat = lift(transfer_up[0, height - 1], level_group)
    low_bit = gz_index & 1
    leaf_slots = jnp.stack([2 * low_bit, 2 * low_bit + 1])
    leaf_others = jnp.take(children, jnp.asarray(SIBLINGS)[leaf_slots], axis=0)
    far_leaf = jnp.einsum(
        "njrs,njsc->nrc", leaf_coupling, leaf_others, preferred_element_type=jnp.float32
    )
    up_piece = lax.dynamic_slice_in_dim(transfer_up[0, middle], gy_index * rank_size, rank_size, 0)
    all_hats, all_pieces = (
        lax.all_gather(node_hat[None], ("gx", "gy"), axis=0, tiled=True),
        lax.all_gather(up_piece[None], ("gx", "gy"), axis=0, tiled=True),
    )
    grouped = all_hats.reshape(lax.axis_size("gx"), lax.axis_size("gy"), rank_size, columns)
    across = lax.dynamic_index_in_dim(grouped, gx_index, 0, keepdims=False)
    far_node = couple_one(across, gy_index, node_coupling[0, middle - 1])
    grouped_pieces = all_pieces.reshape(
        lax.axis_size("gx"), lax.axis_size("gy"), rank_size, rank_size
    )
    top_hats = jnp.einsum(
        "pckr,pckn->prn", grouped_pieces, grouped, preferred_element_type=jnp.float32
    ).astype(jnp.bfloat16)
    far_top = couple_one(top_hats, gx_index, node_coupling[0, middle])
    down_block = lax.dynamic_slice_in_dim(
        transfer_down[0, middle], gy_index * rank_size, rank_size, 0
    )
    down_value = far_node + jnp.dot(
        down_block, far_top.astype(jnp.bfloat16), preferred_element_type=jnp.float32
    )
    height = 1
    slot_index = gz_index >> 2 * height - 1 & 3
    down_block = lax.dynamic_slice_in_dim(
        transfer_down[0, height], slot_index * rank_size, rank_size, 0
    )
    down_value = far_mid[height - 1] + jnp.dot(
        down_block, down_value.astype(jnp.bfloat16), preferred_element_type=jnp.float32
    )
    lowers = transfer_down[0, 0].reshape(4, rank_size, rank_size)
    leaf_blocks = jnp.take(lowers, leaf_slots, axis=0)
    down_leaf = far_leaf + jnp.einsum(
        "nrs,sc->nrc",
        leaf_blocks,
        down_value.astype(jnp.bfloat16),
        preferred_element_type=jnp.float32,
    )
    lowered = down_leaf.astype(jnp.bfloat16)
    tree_out = jnp.einsum("nlk,nkc->nlc", near, rounded, preferred_element_type=jnp.float32)
    tree_out = tree_out + jnp.einsum(
        "nlr,nrc->nlc", basis_out, lowered, preferred_element_type=jnp.float32
    )
    tree_out = tree_out.reshape(rows_here, columns) + ridge[0] * ordered
    inverse = (
        jnp.zeros((rows_here,), jnp.int32)
        .at[local_rows]
        .set(jnp.arange(rows_here, dtype=jnp.int32))
    )
    return jnp.take(tree_out, inverse, axis=0)


def solution(mesh):
    placed = (
        P(("gx", "gy", "gz"), None),
        P(("gx", "gy", "gz")),
        P(("gx", "gy", "gz"), None, None),
        P(("gx", "gy", "gz"), None, None),
        P(("gx", "gy", "gz"), None, None),
        P(("gx", "gy", "gz"), None, None, None),
        P(("gx", "gy", "gz"), None, None, None),
        P(("gx", "gy", "gz"), None, None, None),
        P(("gx", "gy", "gz"), None, None, None, None),
        P(),
    )
    return jax.shard_map(
        on_device,
        mesh=mesh,
        in_specs=placed,
        out_specs=P(("gx", "gy", "gz"), None),
        check_vma=False,
    )
```

profile of v0, /device:TPU:1, one launch (start us, length us, event | category | flops | bytes accessed | tf_op | source)
XLA Modules:
  0.0 215.7 jit_solution(2136695648263740953)
XLA Ops:
  7.4 11.7 %gather_fusion.3 = f32[2048,512]{1,0:T(8,128)} fusion(f32[2048,512]{1,0:T(8,128)} %param.15, s32[2048]{0:T(1024)S(1)} %broadcast_clamp_fusion), kind=kCustom, calls=%fused_computation.clone | custom fusion | bytes 8396800 | tf_op jit(solution)/shard_map/jit(_take)/gather | solution.py:55
  19.0 2.5 %select_convert_fusion = bf16[2048,512]{1,0:T(8,128)(2,1)S(1)} fusion(f32[2048,512]{1,0:T(8,128)} %gather_fusion.3, pred[2048]{0:T(1024)(128)(4,1)S(1)} %get-tuple-element.13), kind=kLoop, calls=%fused_computation.13 | loop fusion | flops 1048576 | bytes 6293504 | tf_op jit(solution)/shard_map/convert_element_type | solution.py:56
  25.2 1.5 collective-permute-done
  27.0 1.5 fusion.19
  29.9 6.2 %collective-permute-done.1 = bf16[1,256,512]{2,1,0:T(8,128)(2,1)S(1)} collective-permute-done((bf16[1,256,512]{2,1,0:T(8,128)(2,1)S(1)}, bf16[1,256,512]{2,1,0:T(8,128)(2,1)S(1)}, u32[]{:S(2)}, u32[]{:S(2)}) %collective-permute-start.1) | collective-permute-done | bytes 262176 | tf_op jit(solution)/shard_map/ppermute | solution.py:13
  37.0 2.8 %collective-permute-start.2 = (bf16[2,256,512]{2,1,0:T(8,128)(2,1)}, bf16[2,256,512]{2,1,0:T(8,128)(2,1)S(1)}, u32[]{:S(2)}, u32[]{:S(2)}) collective-permute-start(bf16[2,256,512]{2,1,0:T(8,128)(2,1)} %pad_maximum_fusion.2), channel_id=1, source_target_pairs={{0,4},{1,5},{2,6},{3,7},{4,0},{5,1},{6,2},{7,3},{8,12},{9,13},{10,... | collective-permute-start | bytes 1572872 | tf_op jit(solution)/shard_map/ppermute | solution.py:13
  39.8 11.1 %collective-permute-done.2 = bf16[2,256,512]{2,1,0:T(8,128)(2,1)S(1)} collective-permute-done((bf16[2,256,512]{2,1,0:T(8,128)(2,1)}, bf16[2,256,512]{2,1,0:T(8,128)(2,1)S(1)}, u32[]{:S(2)}, u32[]{:S(2)}) %collective-permute-start.2) | collective-permute-done | bytes 524320 | tf_op jit(solution)/shard_map/ppermute | solution.py:13
  51.1 2.2 %fusion.20 = bf16[256,512]{0,1:T(8,128)(2,1)} fusion(bf16[1024,512]{1,0:T(8,128)(2,1)S(1)} %bitcast.113, bf16[1,3,1024,256]{3,2,1,0:T(8,128)(2,1)} %param.21), kind=kOutput, calls=%fused_computation.37 | convolution fusion | flops 268566528 | bytes 1835008 | tf_op jit(solution)/shard_map/kr,kc->rc/dot_general | solution.py:31
  53.4 1.9 slice.34
  55.3 1.6 constant_dynamic-slice_fusion.1
  57.6 2.5 %fusion.73 = (bf16[1,1,1024,256]{3,2,1,0:T(8,128)(2,1)}, bf16[1,1,1024,256]{3,2,1,0:T(8,128)(2,1)}, bf16[1,1,1024,256]{3,2,1,0:T(8,128)(2,1)}) fusion(bf16[1,3,1024,256]{3,2,1,0:T(8,128)(2,1)} %param.22), kind=kLoop, calls=%fused_computation.119 | loop fusion | bytes 3145728 | tf_op jit(solution)/shard_map/slice | solution.py:106
  60.1 1.6 gather_fusion.2
  62.4 8.0 %scatter_custom_fusion = s32[2048]{0:T(1024)S(1)} fusion(s32[2048]{0:T(1024)S(1)} %get-tuple-element.14, s32[2048]{0:T(1024)S(1)} %iota.3, s32[]{:T(128)} %constant.60.clone.1), kind=kCustom, calls=%fused_computation.89 | custom fusion | bytes 8196 | tf_op jit(solution)/shard_map/scatter | solution.py:123
  70.6 7.4 %fusion.74 = f32[2,512,1024]{2,1,0:T(8,128)} fusion(bf16[2,1024,512]{2,1,0:T(8,128)(2,1)} %bitcast.116, bf16[2,1024,1024]{2,1,0:T(8,128)(2,1)} %param.17), kind=kOutput, calls=%fused_computation.120 | convolution fusion | flops 2147483648 | bytes 10485760 | tf_op jit(solution)/shard_map/nlk,nkc->nlc/dot_general | solution.py:115
  78.1 1.8 gather_fusion.1
  79.9 2.6 %copy.20 = bf16[2,3,256,512]{2,3,1,0:T(8,128)(2,1)} copy(bf16[2,3,256,512]{3,2,1,0:T(8,128)(2,1)} %bitcast.112) | data formatting | bytes 3145728 | tf_op jit(solution)/shard_map/jit(_take)/gather | solution.py:73
  82.6 3.2 %fusion.10 = f32[2,256,512]{1,2,0:T(8,128)} fusion(bf16[2,3,256,256]{3,2,1,0:T(8,128)(2,1)} %param.20, bf16[2,3,256,512]{2,3,1,0:T(8,128)(2,1)} %copy.20, pred[2,3]{1,0:T(4,128)(4,1)S(1)} %compare_and_fusion.6), kind=kOutput, calls=%fused_computation.20 | convolution fusion | flops 403439616 | bytes 3407878 | tf_op jit(solution)/shard_map/njrs,njsc->nrc/dot_general | solution.py:74
  86.4 2.3 %convolution_bitcast_fusion.2 = f32[256,512]{0,1:T(8,128)} fusion(bf16[3,256,512]{2,1,0:T(8,128)(2,1)S(1)} %gather_fusion.4, pred[3]{0:T(512)(128)(4,1)S(1)} %get-tuple-element.24, bf16[1,3,3,256,256]{4,3,2,1,0:T(8,128)(2,1)} %param.23), kind=kOutput, calls=%fused_computation.27 | convolution fusion | flops 201719808 | bytes 1703939 | tf_op jit(solution)/shard_map/jrs,jsc->rc/dot_general | solution.py:26
  88.7 25.6 %all-gather.5.cloned.1.call-done = bf16[4096,512]{0,1:T(8,128)(2,1)} async-done(((bf16[256,512]{0,1:T(8,128)(2,1)}), bf16[4096,512]{0,1:T(8,128)(2,1)}) %all-gather.5.cloned.1.call-update) | async-done | bytes 4194320 | tf_op jit(solution)/shard_map/all_gather | solution.py:79
  114.3 7.9 %reshape.150 = bf16[4,4,256,512]{2,1,0,3:T(4,128)(2,1)} reshape(bf16[4096,512]{0,1:T(8,128)(2,1)} %all-gather.5.cloned.1.call-done) | data formatting | bytes 8388608 | tf_op jit(solution)/shard_map/reshape | solution.py:82
  122.2 1.6 constant_dynamic-slice_fusion.3
  124.7 36.1 %all-gather.7.cloned.1.call-done = bf16[16,1,256,256]{3,2,1,0:T(8,128)(2,1)} async-done(((bf16[1,1,256,256]{3,2,1,0:T(8,128)(2,1)}), bf16[16,1,256,256]{3,2,1,0:T(8,128)(2,1)}) %all-gather.7.cloned.1.call-update) | async-done | bytes 2097168 | tf_op jit(solution)/shard_map/all_gather | solution.py:80
  160.8 6.9 %bitcast_convert_fusion = bf16[4,256,512]{2,1,0:T(8,128)(2,1)} fusion(bf16[4,4,256,512]{2,1,0,3:T(4,128)(2,1)} %reshape.150, bf16[4,4,256,256]{3,2,1,0:T(8,128)(2,1)} %bitcast.118), kind=kOutput, calls=%fused_computation.15 | convolution fusion | flops 1074266112 | bytes 7340032 | tf_op jit(solution)/shard_map/pckr,pckn->prn/dot_general | solution.py:88
  167.7 1.5 gather_fusion.5
  169.2 2.6 %convolution_bitcast_fusion.1 = f32[256,512]{0,1:T(8,128)} fusion(bf16[3,256,512]{2,1,0:T(8,128)(2,1)} %gather_fusion.5, pred[3]{0:T(512)(128)(4,1)S(1)} %get-tuple-element.26, bf16[1,3,3,256,256]{4,3,2,1,0:T(8,128)(2,1)} %param.23), kind=kOutput, calls=%fused_computation.26 | convolution fusion | flops 201719808 | bytes 1703939 | tf_op jit(solution)/shard_map/jrs,jsc->rc/dot_general | solution.py:26
  171.8 1.8 gather_fusion.6
  173.7 2.6 %fusion.16 = bf16[256,512]{0,1:T(8,128)(2,1)} fusion(f32[256,512]{0,1:T(8,128)} %convolution_bitcast_fusion.1, bf16[3,256,512]{2,1,0:T(8,128)(2,1)S(1)} %gather_fusion.6, pred[3]{0:T(512)(128)(4,1)S(1)} %get-tuple-element.6, bf16[1,3,3,256,256]{4,3,2,1,0:T(8,128)(2,1)} %param.23, bf16[1,1,1024,256]{3,2,1,0:T(8,128)(2,1)} %get-tuple-element.16, ...), kind=kOutput, calls=%fused_computation.33 | convolution fusion | flops 269221888 | bytes 2097159 | tf_op jit(solution)/shard_map/dot_general | solution.py:95
  177.7 5.1 %add_bitcast_fusion = f32[2,1024,512]{1,2,0:T(8,128)} fusion(f32[2,512,1024]{2,1,0:T(8,128)} %fusion.74, bf16[2,1024,256]{2,1,0:T(8,128)(2,1)S(1)} %copy-done, f32[2,256,512]{1,2,0:T(8,128)S(1)} %copy-done.2, bf16[256,512,1]{0,1,2:T(8,128)(2,1)S(1)} %fusion.18, bf16[2,256,256]{2,1,0:T(8,128)(2,1)S(1)} %gather_fusion.2, pred[2]{0:T(512)(128)(4,1)S(1)} %compare_and_fusion.5), kind=kOutput, calls=%fused_computation.12 | convolution fusion | flops 672792576 | bytes 11010050 | tf_op jit(solution)/shard_map/nlr,nrc->nlc/dot_general | solution.py:116
  182.8 5.4 %copy.31 = f32[2,1024,512]{2,1,0:T(8,128)} copy(f32[2,1024,512]{1,2,0:T(8,128)} %add_bitcast_fusion) | data formatting | bytes 8388608 | tf_op jit(solution)/shard_map/add | solution.py:116
  188.3 5.1 %bitcast_add_fusion = f32[2048,512]{1,0:T(8,128)} fusion(f32[2,1024,512]{2,1,0:T(8,128)} %copy.31, f32[2048,512]{1,0:T(8,128)} %gather_fusion.3, f32[]{:T(128)} %bitcast.110, pred[2048]{0:T(1024)(128)(4,1)S(1)} %get-tuple-element.13), kind=kLoop, calls=%fused_computation.9 | loop fusion | flops 3145728 | bytes 12584964 | tf_op jit(solution)/shard_map/add | solution.py:119
  193.3 11.7 %gather_fusion.7 = f32[2048,512]{1,0:T(8,128)} fusion(f32[2048,512]{1,0:T(8,128)} %bitcast_add_fusion, s32[2048]{0:T(1024)S(1)} %fusion.57), kind=kCustom, calls=%fused_computation.2.clone | custom fusion | bytes 8396800 | tf_op jit(solution)/shard_map/jit(_take)/gather | solution.py:125
  205.1 3.8 %broadcast_select_fusion = f32[2048,512]{1,0:T(8,128)} fusion(f32[2048,512]{1,0:T(8,128)} %gather_fusion.7, pred[2048]{0:T(1024)(128)(4,1)S(1)} %compare_and_fusion), kind=kLoop, calls=%fused_computation.16 | loop fusion | flops 1048576 | bytes 8390656 | tf_op jit(solution)/shard_map/jit(_take)/select_n | solution.py:125
  (42 shorter events, 11.0 us)
Async XLA Ops:
  6.5 171.2 %copy-start = (bf16[2,1024,256]{2,1,0:T(8,128)(2,1)S(1)}, bf16[2,1024,256]{2,1,0:T(8,128)(2,1)}, u32[]{:S(2)}) copy-start(bf16[2,1024,256]{2,1,0:T(8,128)(2,1)} %param.19) | copy-start | bytes 3145732
  6.5 107.7 %all-gather.5.cloned.1.call-start = ((), (), s32[]{:S(2)}) async-start(), calls=%async_computation | async-start | bytes 4456448 | tf_op jit(solution)/shard_map/all_gather | solution.py:79
  19.0 3.9 %copy-start.4 = (bf16[2,1024,256]{2,1,0:T(8,128)(2,1)S(1)}, bf16[2,1024,256]{2,1,0:T(8,128)(2,1)}, u32[]{:S(2)}) copy-start(bf16[2,1024,256]{2,1,0:T(8,128)(2,1)} %param.18) | copy-start | bytes 3145732
  21.6 1.4 copy-start.1
  23.7 3.0 %collective-permute-start = (bf16[2,256,512]{2,1,0:T(8,128)(2,1)S(1)}, bf16[2,256,512]{2,1,0:T(8,128)(2,1)S(1)}, u32[]{:S(2)}, u32[]{:S(2)}) collective-permute-start(bf16[2,256,512]{2,1,0:T(8,128)(2,1)S(1)} %fusion.14), channel_id=1, source_target_pairs={{0,1},{1,0},{2,3},{3,2},{4,5},{5,4},{6,7},{7,6},{8,9},{9,8},{10,11... | collective-permute-start | bytes 1572872 | tf_op jit(solution)/shard_map/ppermute | solution.py:13
  28.5 7.6 %collective-permute-start.1 = (bf16[1,256,512]{2,1,0:T(8,128)(2,1)S(1)}, bf16[1,256,512]{2,1,0:T(8,128)(2,1)S(1)}, u32[]{:S(2)}, u32[]{:S(2)}) collective-permute-start(bf16[1,256,512]{2,1,0:T(8,128)(2,1)S(1)} %fusion.19), channel_id=1, source_target_pairs={{0,2},{1,3},{2,0},{3,1},{4,6},{5,7},{6,4},{7,5},{8,10},{9,11},{10,... | collective-permute-start | bytes 786440 | tf_op jit(solution)/shard_map/ppermute | solution.py:13
  37.0 13.9 %collective-permute-start.2 = (bf16[2,256,512]{2,1,0:T(8,128)(2,1)}, bf16[2,256,512]{2,1,0:T(8,128)(2,1)S(1)}, u32[]{:S(2)}, u32[]{:S(2)}) collective-permute-start(bf16[2,256,512]{2,1,0:T(8,128)(2,1)} %pad_maximum_fusion.2), channel_id=1, source_target_pairs={{0,4},{1,5},{2,6},{3,7},{4,0},{5,1},{6,2},{7,3},{8,12},{9,13},{10,... | collective-permute-start | bytes 1572872 | tf_op jit(solution)/shard_map/ppermute | solution.py:13
  39.8 17.1 %copy-start.3 = (s32[4,3]{1,0:T(4,128)S(1)}, s32[4,3]{1,0:T(4,128)}, u32[]{:S(2)}) copy-start(s32[4,3]{1,0:T(4,128)} %constant.98.clone) | copy-start | bytes 148
  53.3 107.4 %all-gather.7.cloned.1.call-start = ((), (), s32[]{:S(2)}) async-start(), calls=%async_computation.1 | async-start | bytes 2228224 | tf_op jit(solution)/shard_map/all_gather | solution.py:80
  169.2 8.5 %copy-start.2 = (f32[2,256,512]{1,2,0:T(8,128)S(1)}, f32[2,256,512]{1,2,0:T(8,128)}, u32[]{:S(2)}) copy-start(f32[2,256,512]{1,2,0:T(8,128)} %fusion.10) | copy-start | bytes 3145732
Sparse Core Ops, SparseCore 0:
  53.5 60.7 all-gather.4
  116.4 44.3 all-gather.6
where the time goes:
time: 217 us; the launch traced here: 216 us
  waiting for transfers between devices  80.6 us (37%)
  local copies, waits for them, and re-layouts  65.3 us (30%)
  matrix products  36.1 us (17%)
  between operations  14.3 us (7%)
  other arithmetic  13.7 us (6%)
  starting transfers between devices  5.75 us (3%)
    all_gather x1, waiting for transfers between devices, on_device(): lax.all_gather(up_piece[None], ('gx', 'gy'), axis=0, tiled=True)  36.1 us
    all_gather x1, waiting for transfers between devices, on_device(): lax.all_gather(node_hat[None], ('gx', 'gy'), axis=0, tiled=True)  25.6 us
    ppermute x3, waiting for transfers between devices, from_partner(): return lax.ppermute(value, axis, pairs)  18.9 us
    gather x1, local copies, waits for them, and re-layouts, on_device(): return jnp.take(tree_out, inverse, axis=0)  11.7 us
    gather x1, local copies, waits for them, and re-layouts, on_device(): ordered = jnp.take(points, local_rows, axis=0)  11.7 us
    scatter x1, local copies, waits for them, and re-layouts, on_device(): inverse = jnp.zeros((rows_here,), jnp.int32).at[local_rows].set(jnp.arang...  8.05 us
    reshape x1, local copies, waits for them, and re-layouts, on_device(): all_hats.reshape(lax.axis_size('gx'), lax.axis_size('gy'), rank_size, col...  7.89 us
    dot_general x1, matrix products, on_device(): jnp.einsum('nlk,nkc->nlc', near, rounded, preferred_element_type=jnp.floa...  7.44 us
  transfers between devices with their start and end apart: 5, of which 5 were waited for; matrix products, arithmetic and copies ran while one was open for 21% of the time, Pallas kernels for 0%

commit v1 on v0

v1 whole, which is shorter than its diff:
```python
import jax
import jax.numpy as jnp
from jax import lax
from jax.experimental import pallas as pl
from jax.experimental.pallas import tpu as pltpu
from jax.sharding import PartitionSpec as P

F32 = jnp.float32
BF16 = jnp.bfloat16
MESH = pl.DeviceIdType.MESH

ROWS = 2048
LEAF = 1024
COLS = 512
RANK = 256
HALF = 256
PART = 64
TILES = ROWS // 8
LANES = COLS // 128
FLAT = ROWS * LANES
BATCH = 16
UNROLL = 64


def nt(a, b):
    return lax.dot_general(a, b, (((1,), (1,)), ((), ())), preferred_element_type=F32)


def nn(a, b):
    return jnp.dot(a, b, preferred_element_type=F32)


def row_places(order):
    local = order & (ROWS - 1)
    return ((local >> 3) << 5) + (local & 7)


def place_of(places, step, u):
    return places[step >> 1, (step & 1) * UNROLL + u]


def tree_kernel(
    order,
    ridge,
    points,
    near,
    basis_in,
    leaf_coupling,
    transfer_up,
    transfer_down,
    node_coupling,
    acc,
    low0,
    pts_v,
    near_v,
    basis_v,
    lc_v,
    up_v,
    dn1_v,
    dn2_v,
    dn3_v,
    nc_v,
    place_v,
    place_s,
    rounded,
    hat0,
    sib0,
    hat1,
    all1,
    hat2,
    all2,
    hat3,
    all3,
    far0,
    far1,
    low2,
    low1,
    load_sem,
    point_sem,
    place_sem,
    a_send,
    a_recv,
    b_send,
    b_recv,
    b2_send,
    b2_recv,
    c_send,
    c_recv,
    d_send,
    d_recv,
    e_send,
    e_recv,
    f_send,
    f_recv,
):
    gx = lax.axis_index("gx")
    gy = lax.axis_index("gy")
    gz = lax.axis_index("gz")
    x = gz // 2
    k = lax.rem(gz, 2)
    twin = (gx, gy, x * 2 + (1 - k))
    on_x = [None] + [(gx, gy, lax.rem(x + j, 4) * 2 + k) for j in (1, 2, 3)]
    on_y = [None] + [(gx, lax.rem(gy + j, 4), gz) for j in (1, 2, 3)]
    on_g = [None] + [(lax.rem(gx + j, 4), gy, gz) for j in (1, 2, 3)]

    barrier = pltpu.get_barrier_semaphore()
    for dev in [twin] + on_x[1:] + on_y[1:] + on_g[1:]:
        pl.semaphore_signal(barrier, inc=1, device_id=dev, device_id_type=MESH)

    chunk = FLAT // 4
    point_copies = [
        pltpu.make_async_copy(
            points.at[pl.ds(i * chunk, chunk)],
            pts_v.at[pl.ds(i * chunk, chunk)],
            point_sem.at[i],
        )
        for i in range(4)
    ]
    for c in point_copies:
        c.start()
    place_v[...] = row_places(order[...])
    place_copy = pltpu.make_async_copy(place_v, place_s, place_sem)
    place_copy.start()

    def rank_rows(i):
        return pl.ds(pl.multiple_of(i * RANK, RANK), RANK)

    loads = [
        pltpu.make_async_copy(basis_in, basis_v, load_sem.at[0]),
        pltpu.make_async_copy(transfer_up.at[0], up_v, load_sem.at[1]),
        pltpu.make_async_copy(near, near_v, load_sem.at[2]),
        pltpu.make_async_copy(leaf_coupling, lc_v, load_sem.at[3]),
        pltpu.make_async_copy(node_coupling.at[0], nc_v, load_sem.at[4]),
        pltpu.make_async_copy(
            transfer_down.at[0, 0, pl.ds(pl.multiple_of(k * 2 * RANK, 2 * RANK), 2 * RANK)],
            dn1_v,
            load_sem.at[5],
        ),
        pltpu.make_async_copy(transfer_down.at[0, 1, rank_rows(x)], dn2_v, load_sem.at[6]),
        pltpu.make_async_copy(transfer_down.at[0, 2, rank_rows(gy)], dn3_v, load_sem.at[7]),
    ]
    place_copy.wait()
    for c in point_copies:
        c.wait()
    for c in loads:
        c.start()

    def gather(step, _):
        for w in range(UNROLL // BATCH):
            rows = []
            for u in range(w * BATCH, (w + 1) * BATCH):
                rows.append(pts_v[pl.ds(place_of(place_s, step, u), LANES, stride=8), :])
            for u in range(w * BATCH, (w + 1) * BATCH):
                to = step * (UNROLL * LANES) + (u // 8) * 32 + (u % 8)
                acc[pl.ds(to, LANES, stride=8), :] = rows[u - w * BATCH]
        return 0

    lax.fori_loop(0, ROWS // UNROLL, gather, 0)
    acc4 = acc.reshape(TILES, LANES, 8, 128)

    def to_bf16(step, _):
        for c in range(LANES):
            block = acc4[pl.ds(step * 16, 16), c]
            rounded[pl.ds(step * 128, 128), c * 128 : (c + 1) * 128] = block.reshape(128, 128).astype(BF16)
        return 0

    lax.fori_loop(0, ROWS // 128, to_bf16, 0)

    loads[0].wait()
    for leaf in range(2):
        hat0[leaf] = lax.dot_general(
            rounded[leaf * LEAF : (leaf + 1) * LEAF],
            basis_v[leaf],
            (((0,), (0,)), ((), ())),
            preferred_element_type=F32,
        ).astype(BF16)
    pl.semaphore_wait(barrier, 10)

    mine = pl.ds(pl.multiple_of(k * HALF, HALF), HALF)
    other = pl.ds(pl.multiple_of((1 - k) * HALF, HALF), HALF)

    def remote(src, dst, send, recv, dev):
        return pltpu.make_async_remote_copy(
            src_ref=src, dst_ref=dst, send_sem=send, recv_sem=recv, device_id=dev, device_id_type=MESH
        )

    a_copies = [
        remote(hat0.at[:, rows], sib0.at[:, rows], a_send.at[i], a_recv.at[i], twin)
        for i, rows in enumerate((other, mine))
    ]
    a_copies[0].start()
    a_copies[1].start()

    gain = ridge[0]
    loads[2].wait()

    def near_chunk(i):
        leaf, q = i // 4, i % 4
        block = nn(near_v[leaf, q * 256 : (q + 1) * 256], rounded[leaf * LEAF : (leaf + 1) * LEAF])
        t = leaf * 128 + q * 32
        for c in range(LANES):
            acc4[t : t + 32, c] = acc4[t : t + 32, c] * gain + block[:, c * 128 : (c + 1) * 128].reshape(32, 8, 128)

    loads[1].wait()
    total1 = nn(hat0[0, mine], up_v[0, rank_rows(2 * k)]) + nn(hat0[1, mine], up_v[0, rank_rows(2 * k + 1)])
    near_chunk(0)
    near_chunk(1)
    remote(hat0.at[:, other], sib0.at[:, mine], a_send.at[0], a_recv.at[0], twin).wait_recv()
    sib = 1 - k
    total1 += nn(sib0[0, mine], up_v[0, rank_rows(2 * sib)]) + nn(sib0[1, mine], up_v[0, rank_rows(2 * sib + 1)])
    value1 = total1.astype(BF16)
    hat1[0:HALF] = value1
    hat1[HALF : 2 * HALF] = value1
    b_copies, b2_copies = [None], [None]
    for j in (1, 2, 3):
        start = lax.rem(x + j, 4) * PART
        b_copies.append(
            remote(
                hat1.at[pl.ds(pl.multiple_of(start, PART), PART)],
                all1.at[x, 0:PART],
                b_send.at[j - 1],
                b_recv.at[j - 1],
                on_x[j],
            )
        )
        b2_copies.append(
            remote(
                hat1.at[pl.ds(pl.multiple_of(start + PART, PART), 3 * PART)],
                all1.at[x, PART:HALF],
                b2_send.at[j - 1],
                b2_recv.at[j - 1],
                on_x[j],
            )
        )
    for j in (2, 1, 3):
        b_copies[j].start()
    for j in (2, 1, 3):
        b2_copies[j].start()

    total2 = nn(hat1[pl.ds(pl.multiple_of(x * PART, PART), PART)], up_v[1, rank_rows(x)])
    near_chunk(2)
    near_chunk(3)
    near_chunk(4)
    for j in (1, 3, 2):
        s = lax.rem(x - j + 4, 4)
        b_copies[j].wait_recv()
        total2 += nn(all1[s, 0:PART], up_v[1, rank_rows(s)])
    hat2[...] = total2.astype(BF16)
    c_copies = [None] + [
        remote(hat2, all2.at[gy], c_send.at[j - 1], c_recv.at[j - 1], on_y[j]) for j in (1, 2, 3)
    ]
    for j in (2, 1, 3):
        c_copies[j].start()

    total3 = nn(hat2[...], up_v[2, rank_rows(gy)])
    near_chunk(5)
    near_chunk(6)
    near_chunk(7)
    for j in (1, 3, 2):
        s = lax.rem(gy - j + 4, 4)
        c_copies[j].wait_recv()
        total3 += nn(all2[s], up_v[2, rank_rows(s)])
    hat3[...] = total3.astype(BF16)
    d_copies = [None] + [
        remote(hat3, all3.at[gx], d_send.at[j - 1], d_recv.at[j - 1], on_g[j]) for j in (1, 2, 3)
    ]
    for j in (2, 1, 3):
        d_copies[j].start()

    def skip(s, own):
        return jnp.where(s > own, s - 1, s)

    loads[3].wait()
    loads[4].wait()
    far2 = jnp.zeros((PART, RANK), F32)
    for j in (1, 2, 3):
        s = lax.rem(gy - j + 4, 4)
        far2 += nt(all2[s], nc_v[1, skip(s, gy)])
    a_copies[1].wait_recv()
    for leaf in range(2):
        far0[leaf] = (
            nt(hat0[1 - leaf], lc_v[leaf, 2 * k])
            + nt(sib0[0], lc_v[leaf, 1 - k])
            + nt(sib0[1], lc_v[leaf, 2 - k])
        )
    far3 = jnp.zeros((PART, RANK), F32)
    for j in (1, 3, 2):
        s = lax.rem(gx - j + 4, 4)
        d_copies[j].wait_recv()
        far3 += nt(all3[s], nc_v[2, skip(s, gx)])

    loads[7].wait()
    value2 = (far2 + nt(far3.astype(BF16), dn3_v[...])).astype(BF16)
    low2[0:PART] = value2
    e_copies = [None] + [
        remote(
            low2.at[0:PART],
            low2.at[(4 - j) * PART : (5 - j) * PART],
            e_send.at[j - 1],
            e_recv.at[j - 1],
            on_x[j],
        )
        for j in (1, 2, 3)
    ]
    for j in (2, 1, 3):
        e_copies[j].start()
    total = jnp.zeros((HALF, RANK), F32)
    for j in (1, 2, 3):
        s = lax.rem(x - j + 4, 4)
        b2_copies[j].wait_recv()
        total += nt(all1[s], nc_v[0, skip(s, x)])
    far1[...] = total
    loads[6].wait()
    for m in (0, 3, 1, 2):
        if m:
            e_copies[4 - m].wait_recv()
        value = far1[m * PART : (m + 1) * PART] + nt(low2[m * PART : (m + 1) * PART], dn2_v[...])
        to = k * HALF + lax.rem(x + m, 4) * PART
        low1[pl.ds(pl.multiple_of(to, PART), PART)] = value.astype(BF16)
    f_copy = remote(low1.at[mine], low1.at[mine], f_send, f_recv, twin)
    f_copy.start()
    loads[5].wait()

    def leaf_down(rows):
        for leaf in range(2):
            value = far0[leaf, rows] + nt(low1[rows], dn1_v[leaf * RANK : (leaf + 1) * RANK])
            low0[leaf, rows] = value.astype(BF16)

    leaf_down(mine)
    remote(low1.at[other], low1.at[other], f_send, f_recv, twin).wait_recv()
    leaf_down(other)

    for c in a_copies + b_copies[1:] + b2_copies[1:] + c_copies[1:] + d_copies[1:] + e_copies[1:] + [f_copy]:
        c.wait_send()


def leaf_kernel(order, acc, basis_out, low0, out, place_v, place_s, fin, out_v, place_sem, out_sem):
    place_v[...] = row_places(order[...])
    place_copy = pltpu.make_async_copy(place_v, place_s, place_sem)
    place_copy.start()
    acc4 = acc.reshape(TILES, LANES, 8, 128)
    fin4 = fin.reshape(TILES, LANES, 8, 128)
    for i in range(8):
        leaf, q = i // 4, i % 4
        block = nt(basis_out[leaf, q * 256 : (q + 1) * 256], low0[leaf])
        t = leaf * 128 + q * 32
        for c in range(LANES):
            fin4[t : t + 32, c] = acc4[t : t + 32, c] + block[:, c * 128 : (c + 1) * 128].reshape(32, 8, 128)
    place_copy.wait()

    def scatter(step, _):
        for w in range(UNROLL // BATCH):
            rows = []
            for u in range(w * BATCH, (w + 1) * BATCH):
                at = step * (UNROLL * LANES) + (u // 8) * 32 + (u % 8)
                rows.append(fin[pl.ds(at, LANES, stride=8), :])
            for u in range(w * BATCH, (w + 1) * BATCH):
                out_v[pl.ds(place_of(place_s, step, u), LANES, stride=8), :] = rows[u - w * BATCH]
        return 0

    lax.fori_loop(0, ROWS // UNROLL, scatter, 0)
    chunk = FLAT // 4
    copies = [
        pltpu.make_async_copy(
            out_v.at[pl.ds(i * chunk, chunk)], out.at[pl.ds(i * chunk, chunk)], out_sem.at[i]
        )
        for i in range(4)
    ]
    for c in copies:
        c.start()
    for c in copies:
        c.wait()


def on_device(
    points,
    order,
    near,
    basis_in,
    basis_out,
    leaf_coupling,
    transfer_up,
    transfer_down,
    node_coupling,
    ridge,
):
    flat_points = points.reshape(TILES, 8, LANES, 128).transpose(0, 2, 1, 3).reshape(FLAT, 128)
    order_rows = order.reshape(ROWS // 128, 128)
    vmem = pl.BlockSpec(memory_space=pltpu.VMEM)
    smem = pl.BlockSpec(memory_space=pltpu.SMEM)
    hbm = pl.BlockSpec(memory_space=pltpu.HBM)
    dma = pltpu.SemaphoreType.DMA
    acc, low0 = pl.pallas_call(
        tree_kernel,
        out_shape=(
            jax.ShapeDtypeStruct((FLAT, 128), F32),
            jax.ShapeDtypeStruct((2, COLS, RANK), BF16),
        ),
        in_specs=[vmem, smem] + [hbm] * 7,
        out_specs=(vmem, vmem),
        scratch_shapes=[
            pltpu.VMEM((FLAT, 128), F32),
            pltpu.VMEM((2, LEAF, LEAF), BF16),
            pltpu.VMEM((2, LEAF, RANK), BF16),
            pltpu.VMEM((2, 3, RANK, RANK), BF16),
            pltpu.VMEM((3, 4 * RANK, RANK), BF16),
            pltpu.VMEM((2 * RANK, RANK), BF16),
            pltpu.VMEM((RANK, RANK), BF16),
            pltpu.VMEM((RANK, RANK), BF16),
            pltpu.VMEM((3, 3, RANK, RANK), BF16),
            pltpu.VMEM((ROWS // 128, 128), jnp.int32),
            pltpu.SMEM((ROWS // 128, 128), jnp.int32),
            pltpu.VMEM((ROWS, COLS), BF16),
            pltpu.VMEM((2, COLS, RANK), BF16),
            pltpu.VMEM((2, COLS, RANK), BF16),
            pltpu.VMEM((2 * HALF, RANK), BF16),
            pltpu.VMEM((4, HALF, RANK), BF16),
            pltpu.VMEM((PART, RANK), BF16),
            pltpu.VMEM((4, PART, RANK), BF16),
            pltpu.VMEM((PART, RANK), BF16),
            pltpu.VMEM((4, PART, RANK), BF16),
            pltpu.VMEM((2, COLS, RANK), F32),
            pltpu.VMEM((HALF, RANK), F32),
            pltpu.VMEM((4 * PART, RANK), BF16),
            pltpu.VMEM((COLS, RANK), BF16),
            dma((8,)),
            dma((4,)),
            dma,
            dma((2,)),
            dma((2,)),
            dma((3,)),
            dma((3,)),
            dma((3,)),
            dma((3,)),
            dma((3,)),
            dma((3,)),
            dma((3,)),
            dma((3,)),
            dma((3,)),
            dma((3,)),
            dma,
            dma,
        ],
        compiler_params=pltpu.CompilerParams(
            collective_id=0, has_side_effects=True, vmem_limit_bytes=54 << 20
        ),
        name="tree",
    )(
        order_rows,
        ridge,
        flat_points,
        near,
        basis_in,
        leaf_coupling,
        transfer_up,
        transfer_down,
        node_coupling,
    )
    out = pl.pallas_call(
        leaf_kernel,
        out_shape=jax.ShapeDtypeStruct((FLAT, 128), F32),
        in_specs=[vmem] * 4,
        out_specs=hbm,
        scratch_shapes=[
            pltpu.VMEM((ROWS // 128, 128), jnp.int32),
            pltpu.SMEM((ROWS // 128, 128), jnp.int32),
            pltpu.VMEM((FLAT, 128), F32),
            pltpu.VMEM((FLAT, 128), F32),
            dma,
            dma((4,)),
        ],
        compiler_params=pltpu.CompilerParams(vmem_limit_bytes=24 << 20),
        name="leaves",
    )(order_rows, acc, basis_out, low0)
    return out.reshape(TILES, LANES, 8, 128).transpose(0, 2, 1, 3).reshape(ROWS, COLS)


def solution(mesh):
    placed = (
        P(("gx", "gy", "gz"), None),
        P(("gx", "gy", "gz")),
        P(("gx", "gy", "gz"), None, None),
        P(("gx", "gy", "gz"), None, None),
        P(("gx", "gy", "gz"), None, None),
        P(("gx", "gy", "gz"), None, None, None),
        P(("gx", "gy", "gz"), None, None, None),
        P(("gx", "gy", "gz"), None, None, None),
        P(("gx", "gy", "gz"), None, None, None, None),
        P(),
    )
    return jax.shard_map(
        on_device,
        mesh=mesh,
        in_specs=placed,
        out_specs=P(("gx", "gy", "gz"), None),
        check_vma=False,
    )
```

time: 217 us -> 48.8 us (0.22)
  waiting for transfers between devices: 80.6 us -> 0 us
  local copies, waits for them, and re-layouts: 65.3 us -> 3.23 us
  Pallas kernels: 0 us -> 44.7 us
  matrix products: 36.1 us -> 0 us
  other arithmetic: 13.7 us -> 0 us
  between operations: 14.3 us -> 0.7 us
  starting transfers between devices: 5.75 us -> 0 us
    all_gather x2 -> x0, waiting for transfers between devices: 61.7 us -> none  [the longest x1 36.1 us: on_device(): lax.all_gather(up_piece[None], ('gx', 'gy'), axis=0, tiled=True)]
    pallas_call x0 -> x2, Pallas kernels: none -> 44.7 us  [the longest x1 36.8 us: on_device(): pl.pallas_call(tree_kernel, out_shape=(jax.ShapeDtypeStruct((FLAT, 128),...]
    dot_general x11 -> x0, matrix products: 36.1 us -> none  [the longest x1 7.44 us: on_device(): jnp.einsum('nlk,nkc->nlc', near, rounded, preferred_element_type=jnp.floa...]
    gather x9 -> x0, local copies, waits for them, and re-layouts: 33.9 us -> none  [the longest x1 11.7 us: on_device(): return jnp.take(tree_out, inverse, axis=0)]
    ppermute x3 -> x0, waiting for transfers between devices: 18.9 us -> none  [from_partner(): return lax.ppermute(value, axis, pairs)]
    scatter x1 -> x0, local copies, waits for them, and re-layouts: 8.05 us -> none  [on_device(): inverse = jnp.zeros((rows_here,), jnp.int32).at[local_rows].set(jnp.arang...]
    reshape x1 -> x0, local copies, waits for them, and re-layouts: 7.89 us -> none  [on_device(): all_hats.reshape(lax.axis_size('gx'), lax.axis_size('gy'), rank_size, col...]
    ppermute x3 -> x0, starting transfers between devices: 5.7 us -> none  [from_partner(): return lax.ppermute(value, axis, pairs)]
  transfers between devices with their start and end apart: 5 -> 0, of which waited for: 5 -> 0; matrix products, arithmetic and copies ran while one was open for 21% -> 0% of each run, Pallas kernels for 0% -> 0%
where the time goes in v1:
time: 48.8 us; the launch traced here: 48.6 us
  Pallas kernels  44.7 us (92%)
  local copies, waits for them, and re-layouts  3.23 us (7%)
  between operations  0.7 us (1%)
    pallas_call x1, Pallas kernels, on_device(): pl.pallas_call(tree_kernel, out_shape=(jax.ShapeDtypeStruct((FLAT, 128),...  36.8 us
    pallas_call x1, Pallas kernels, on_device(): pl.pallas_call(leaf_kernel, out_shape=jax.ShapeDtypeStruct((FLAT, 128), F...  7.88 us
    unnamed x8, local copies, waits for them, and re-layouts  3.23 us

profile of v1, /device:TPU:1, one launch (start us, length us, event | category | flops | bytes accessed | tf_op | source)
XLA Modules:
  0.0 48.6 jit_solution(15674008651221347431)
XLA Ops:
  0.7 0.0 copy-start.1
  0.7 0.0 copy-start.3
  0.7 36.8 %tree.1 = (f32[8192,128]{1,0:T(8,128)}, bf16[2,512,256]{2,1,0:T(8,128)(2,1)}) custom-call(s32[16,128]{1,0:T(8,128)} %bitcast.11, f32[1]{0:T(128)S(6)} %copy.11.ridge, f32[8192,128]{1,0:T(8,128)} %bitcast.13, bf16[2,1024,1024]{2,1,0:T(8,128)(2,1)} %near.1, bf16[2,1024,256]{2,1,0:T(8,128)(2,1)} %basis_in.1, bf16[2,3,256,256]{3,2,1,0:T(8,128)(2,1)} %leaf_coupling.1, ...), custom_call_target="tpu_custom_call" | custom-call | tf_op jit(solution)/shard_map/tree/pallas_call | solution.py:393
  37.5 0.0 copy-done.1
  37.5 0.0 copy-done.3
  37.5 0.0 copy-start
  37.5 2.2 %copy-done = f32[8192,128]{1,0:T(8,128)S(1)} copy-done((f32[8192,128]{1,0:T(8,128)S(1)}, f32[8192,128]{1,0:T(8,128)}, u32[]{:S(2)}) %copy-start) | copy-done | bytes 4194328
  39.7 0.0 copy-start.2
  39.7 1.0 %copy-done.2 = bf16[2,512,256]{2,1,0:T(8,128)(2,1)S(1)} copy-done((bf16[2,512,256]{2,1,0:T(8,128)(2,1)S(1)}, bf16[2,512,256]{2,1,0:T(8,128)(2,1)}, u32[]{:S(2)}) %copy-start.2) | copy-done | bytes 524312
  40.7 7.9 %leaves.1 = f32[8192,128]{1,0:T(8,128)} custom-call(s32[16,128]{1,0:T(8,128)S(1)} %bitcast.12, f32[8192,128]{1,0:T(8,128)S(1)} %copy-done, bf16[2,1024,256]{2,1,0:T(8,128)(2,1)S(1)} %copy-done.1, bf16[2,512,256]{2,1,0:T(8,128)(2,1)S(1)} %copy-done.2), custom_call_target="tpu_custom_call" | custom-call | tf_op jit(solution)/shard_map/leaves/pallas_call | solution.py:459
Async XLA Ops:
  0.7 36.8 %copy-start.1 = (bf16[2,1024,256]{2,1,0:T(8,128)(2,1)S(1)}, bf16[2,1024,256]{2,1,0:T(8,128)(2,1)}, u32[]{:S(2)}) copy-start(bf16[2,1024,256]{2,1,0:T(8,128)(2,1)} %basis_out.1) | copy-start | bytes 3145732
  0.7 36.8 %copy-start.3 = (s32[2048]{0:T(1024)S(1)}, s32[2048]{0:T(1024)}, u32[]{:S(2)}) copy-start(s32[2048]{0:T(1024)} %param.11) | copy-start | bytes 24580
  37.5 2.2 %copy-start = (f32[8192,128]{1,0:T(8,128)S(1)}, f32[8192,128]{1,0:T(8,128)}, u32[]{:S(2)}) copy-start(f32[8192,128]{1,0:T(8,128)} %get-tuple-element.7.acc) | copy-start | bytes 12582916
  39.7 1.0 %copy-start.2 = (bf16[2,512,256]{2,1,0:T(8,128)(2,1)S(1)}, bf16[2,512,256]{2,1,0:T(8,128)(2,1)}, u32[]{:S(2)}) copy-start(bf16[2,512,256]{2,1,0:T(8,128)(2,1)} %get-tuple-element.8.low0) | copy-start | bytes 1572868

commit v2 on v1

--- a/solution.py
+++ b/solution.py
@@ -18,8 +18,10 @@
 TILES = ROWS // 8
 LANES = COLS // 128
 FLAT = ROWS * LANES
+WIDE = 2 * LANES
+GROUP = 128
+GROUPS = ROWS // GROUP
 BATCH = 16
-UNROLL = 64
 
 
 def nt(a, b):
@@ -30,13 +32,36 @@
     return jnp.dot(a, b, preferred_element_type=F32)
 
 
-def row_places(order):
-    local = order & (ROWS - 1)
-    return ((local >> 3) << 5) + (local & 7)
-
-
-def place_of(places, step, u):
-    return places[step >> 1, (step & 1) * UNROLL + u]
+def row_places(index, tiles):
+    return (index >> 3) * (8 * tiles) + (index & 7)
+
+
+def inverse_of(local):
+    high, low = local >> 7, local & 127
+    row_high = lax.broadcasted_iota(jnp.int32, (GROUPS, GROUP), 0)
+    row_low = lax.broadcasted_iota(jnp.int32, (GROUP, GROUP), 0)
+    lane = lax.broadcasted_iota(jnp.int32, (GROUPS, GROUP), 1).astype(F32)
+    total = jnp.zeros((2 * GROUPS, GROUP), F32)
+    for b in range(GROUPS):
+        hit_high = jnp.where(row_high == high[b : b + 1], 1.0, 0.0)
+        hit_low = jnp.where(row_low == low[b : b + 1], 1.0, 0.0).astype(BF16)
+        values = jnp.concatenate([hit_high * float(b), hit_high * lane], axis=0).astype(BF16)
+        total += nt(values, hit_low)
+    return (total[:GROUPS] * float(GROUP) + total[GROUPS:]).astype(jnp.int32) & (ROWS - 1)
+
+
+def move_rows(places, source, target, tiles, target_tiles, first, count):
+    def step(i, _):
+        for w in range(GROUP // BATCH):
+            rows = []
+            for u in range(w * BATCH, (w + 1) * BATCH):
+                rows.append(source[pl.ds(places[i, u], tiles, stride=8), :])
+            for u in range(w * BATCH, (w + 1) * BATCH):
+                to = i * (GROUP * target_tiles) + (u // 8) * (8 * target_tiles) + (u % 8)
+                target[pl.ds(to, tiles, stride=8), :] = rows[u - w * BATCH]
+        return 0
+
+    lax.fori_loop(first, first + count, step, 0)
 
 
 def tree_kernel(
@@ -45,13 +70,17 @@
     points,
     near,
     basis_in,
+    basis_out,
     leaf_coupling,
     transfer_up,
     transfer_down,
     node_coupling,
-    acc,
+    turned,
+    turned_basis,
     low0,
     pts_v,
+    wide,
+    out_basis_v,
     near_v,
     basis_v,
     lc_v,
@@ -60,8 +89,12 @@
     dn2_v,
     dn3_v,
     nc_v,
+    order_v,
+    ridge_s,
     place_v,
     place_s,
+    back_v,
+    back_s,
     rounded,
     hat0,
     sib0,
@@ -75,6 +108,7 @@
     far1,
     low2,
     low1,
+    small_sem,
     load_sem,
     point_sem,
     place_sem,
@@ -118,9 +152,20 @@
     ]
     for c in point_copies:
         c.start()
-    place_v[...] = row_places(order[...])
-    place_copy = pltpu.make_async_copy(place_v, place_s, place_sem)
+    small = [
+        pltpu.make_async_copy(order, order_v, small_sem.at[0]),
+        pltpu.make_async_copy(ridge, ridge_s, small_sem.at[1]),
+    ]
+    for c in small:
+        c.start()
+    small[0].wait()
+    local = order_v[...] & (ROWS - 1)
+    place_v[...] = row_places(local, LANES)
+    place_copy = pltpu.make_async_copy(place_v, place_s, place_sem.at[0])
     place_copy.start()
+    back_v[...] = row_places(inverse_of(local), WIDE)
+    back_copy = pltpu.make_async_copy(back_v, back_s, place_sem.at[1])
+    back_copy.start()
 
     def rank_rows(i):
         return pl.ds(pl.multiple_of(i * RANK, RANK), RANK)
@@ -138,6 +183,7 @@
         ),
         pltpu.make_async_copy(transfer_down.at[0, 1, rank_rows(x)], dn2_v, load_sem.at[6]),
         pltpu.make_async_copy(transfer_down.at[0, 2, rank_rows(gy)], dn3_v, load_sem.at[7]),
+        pltpu.make_async_copy(basis_out, out_basis_v, load_sem.at[8]),
     ]
     place_copy.wait()
     for c in point_copies:
@@ -145,37 +191,18 @@
     for c in loads:
         c.start()
 
-    def gather(step, _):
-        for w in range(UNROLL // BATCH):
-            rows = []
-            for u in range(w * BATCH, (w + 1) * BATCH):
-                rows.append(pts_v[pl.ds(place_of(place_s, step, u), LANES, stride=8), :])
-            for u in range(w * BATCH, (w + 1) * BATCH):
-                to = step * (UNROLL * LANES) + (u // 8) * 32 + (u % 8)
-                acc[pl.ds(to, LANES, stride=8), :] = rows[u - w * BATCH]
-        return 0
-
-    lax.fori_loop(0, ROWS // UNROLL, gather, 0)
-    acc4 = acc.reshape(TILES, LANES, 8, 128)
+    move_rows(place_s, pts_v, wide, LANES, WIDE, 0, GROUPS)
+    wide4 = wide.reshape(TILES, WIDE, 8, 128)
 
     def to_bf16(step, _):
         for c in range(LANES):
-            block = acc4[pl.ds(step * 16, 16), c]
+            block = wide4[pl.ds(step * 16, 16), c]
             rounded[pl.ds(step * 128, 128), c * 128 : (c + 1) * 128] = block.reshape(128, 128).astype(BF16)
         return 0
 
     lax.fori_loop(0, ROWS // 128, to_bf16, 0)
 
     loads[0].wait()
-    for leaf in range(2):
-        hat0[leaf] = lax.dot_general(
-            rounded[leaf * LEAF : (leaf + 1) * LEAF],
-            basis_v[leaf],
-            (((0,), (0,)), ((), ())),
-            preferred_element_type=F32,
-        ).astype(BF16)
-    pl.semaphore_wait(barrier, 10)
-
     mine = pl.ds(pl.multiple_of(k * HALF, HALF), HALF)
     other = pl.ds(pl.multiple_of((1 - k) * HALF, HALF), HALF)
 
@@ -184,14 +211,27 @@
             src_ref=src, dst_ref=dst, send_sem=send, recv_sem=recv, device_id=dev, device_id_type=MESH
         )
 
+    def leaf_up(columns):
+        for leaf in range(2):
+            hat0[leaf, columns] = lax.dot_general(
+                rounded[leaf * LEAF : (leaf + 1) * LEAF, columns],
+                basis_v[leaf],
+                (((0,), (0,)), ((), ())),
+                preferred_element_type=F32,
+            ).astype(BF16)
+
     a_copies = [
         remote(hat0.at[:, rows], sib0.at[:, rows], a_send.at[i], a_recv.at[i], twin)
         for i, rows in enumerate((other, mine))
     ]
+    leaf_up(other)
+    pl.semaphore_wait(barrier, 10)
     a_copies[0].start()
+    leaf_up(mine)
     a_copies[1].start()
 
-    gain = ridge[0]
+    small[1].wait()
+    gain = ridge_s[0]
     loads[2].wait()
 
     def near_chunk(i):
@@ -199,7 +239,30 @@
         block = nn(near_v[leaf, q * 256 : (q + 1) * 256], rounded[leaf * LEAF : (leaf + 1) * LEAF])
         t = leaf * 128 + q * 32
         for c in range(LANES):
-            acc4[t : t + 32, c] = acc4[t : t + 32, c] * gain + block[:, c * 128 : (c + 1) * 128].reshape(32, 8, 128)
+            wide4[t : t + 32, c] = wide4[t : t + 32, c] * gain + block[:, c * 128 : (c + 1) * 128].reshape(32, 8, 128)
+
+    def basis_rows(leaf):
+        none = jnp.zeros((32, 8, 128), F32)
+        for q in range(4):
+            t = leaf * 128 + q * 32
+            for c in range(2):
+                block = out_basis_v[leaf, q * 256 : (q + 1) * 256, c * 128 : (c + 1) * 128]
+                wide4[t : t + 32, LANES + leaf * 2 + c] = block.astype(F32).reshape(32, 8, 128)
+                wide4[t : t + 32, LANES + (1 - leaf) * 2 + c] = none
+
+    def turn(first, count):
+        move_rows(back_s, wide, turned, WIDE, WIDE, first, count)
+
+    turned4 = turned.reshape(TILES, WIDE, 8, 128)
+
+    def turned_to_bf16(first, count):
+        def step(i, _):
+            for c in range(LANES):
+                block = turned4[pl.ds(i * 16, 16), LANES + c]
+                turned_basis[pl.ds(i * 128, 128), c * 128 : (c + 1) * 128] = block.reshape(128, 128).astype(BF16)
+            return 0
+
+        lax.fori_loop(first, first + count, step, 0)
 
     loads[1].wait()
     total1 = nn(hat0[0, mine], up_v[0, rank_rows(2 * k)]) + nn(hat0[1, mine], up_v[0, rank_rows(2 * k + 1)])
@@ -238,9 +301,12 @@
         b2_copies[j].start()
 
     total2 = nn(hat1[pl.ds(pl.multiple_of(x * PART, PART), PART)], up_v[1, rank_rows(x)])
-    near_chunk(2)
-    near_chunk(3)
-    near_chunk(4)
+    for i in range(2, 8):
+        near_chunk(i)
+    loads[8].wait()
+    basis_rows(0)
+    basis_rows(1)
+    back_copy.wait()
     for j in (1, 3, 2):
         s = lax.rem(x - j + 4, 4)
         b_copies[j].wait_recv()
@@ -253,9 +319,7 @@
         c_copies[j].start()
 
     total3 = nn(hat2[...], up_v[2, rank_rows(gy)])
-    near_chunk(5)
-    near_chunk(6)
-    near_chunk(7)
+    turn(0, 7)
     for j in (1, 3, 2):
         s = lax.rem(gy - j + 4, 4)
         c_copies[j].wait_recv()
@@ -283,6 +347,7 @@
             + nt(sib0[0], lc_v[leaf, 1 - k])
             + nt(sib0[1], lc_v[leaf, 2 - k])
         )
+    turn(7, 3)
     far3 = jnp.zeros((PART, RANK), F32)
     for j in (1, 3, 2):
         s = lax.rem(gx - j + 4, 4)
@@ -310,64 +375,49 @@
         b2_copies[j].wait_recv()
         total += nt(all1[s], nc_v[0, skip(s, x)])
     far1[...] = total
+    turn(10, 6)
     loads[6].wait()
+    f_copies = []
     for m in (0, 3, 1, 2):
         if m:
             e_copies[4 - m].wait_recv()
         value = far1[m * PART : (m + 1) * PART] + nt(low2[m * PART : (m + 1) * PART], dn2_v[...])
         to = k * HALF + lax.rem(x + m, 4) * PART
-        low1[pl.ds(pl.multiple_of(to, PART), PART)] = value.astype(BF16)
-    f_copy = remote(low1.at[mine], low1.at[mine], f_send, f_recv, twin)
-    f_copy.start()
+        rows = pl.ds(pl.multiple_of(to, PART), PART)
+        low1[rows] = value.astype(BF16)
+        f_copies.append(remote(low1.at[rows], low1.at[rows], f_send.at[m], f_recv.at[m], twin))
+        f_copies[-1].start()
     loads[5].wait()
 
     def leaf_down(rows):
         for leaf in range(2):
             value = far0[leaf, rows] + nt(low1[rows], dn1_v[leaf * RANK : (leaf + 1) * RANK])
-            low0[leaf, rows] = value.astype(BF16)
+            low0[rows, leaf * RANK : (leaf + 1) * RANK] = value.astype(BF16)
 
     leaf_down(mine)
-    remote(low1.at[other], low1.at[other], f_send, f_recv, twin).wait_recv()
+    turned_to_bf16(0, 16)
+    for m in (0, 3, 1, 2):
+        to = (1 - k) * HALF + lax.rem(x + m, 4) * PART
+        rows = pl.ds(pl.multiple_of(to, PART), PART)
+        remote(low1.at[rows], low1.at[rows], f_send.at[m], f_recv.at[m], twin).wait_recv()
     leaf_down(other)
 
-    for c in a_copies + b_copies[1:] + b2_copies[1:] + c_copies[1:] + d_copies[1:] + e_copies[1:] + [f_copy]:
+    for c in a_copies + b_copies[1:] + b2_copies[1:] + c_copies[1:] + d_copies[1:] + e_copies[1:] + f_copies:
         c.wait_send()
 
 
-def leaf_kernel(order, acc, basis_out, low0, out, place_v, place_s, fin, out_v, place_sem, out_sem):
-    place_v[...] = row_places(order[...])
-    place_copy = pltpu.make_async_copy(place_v, place_s, place_sem)
-    place_copy.start()
-    acc4 = acc.reshape(TILES, LANES, 8, 128)
-    fin4 = fin.reshape(TILES, LANES, 8, 128)
+def leaf_kernel(turned, turned_basis, low0, out, out_v, out_sem):
+    turned4 = turned.reshape(TILES, WIDE, 8, 128)
+    out4 = out_v.reshape(TILES, LANES, 8, 128)
+    copies = []
     for i in range(8):
-        leaf, q = i // 4, i % 4
-        block = nt(basis_out[leaf, q * 256 : (q + 1) * 256], low0[leaf])
-        t = leaf * 128 + q * 32
+        block = nt(turned_basis[i * 256 : (i + 1) * 256], low0[...])
+        t = i * 32
         for c in range(LANES):
-            fin4[t : t + 32, c] = acc4[t : t + 32, c] + block[:, c * 128 : (c + 1) * 128].reshape(32, 8, 128)
-    place_copy.wait()
-
-    def scatter(step, _):
-        for w in range(UNROLL // BATCH):
-            rows = []
-            for u in range(w * BATCH, (w + 1) * BATCH):
-                at = step * (UNROLL * LANES) + (u // 8) * 32 + (u % 8)
-                rows.append(fin[pl.ds(at, LANES, stride=8), :])
-            for u in range(w * BATCH, (w + 1) * BATCH):
-                out_v[pl.ds(place_of(place_s, step, u), LANES, stride=8), :] = rows[u - w * BATCH]
-        return 0
-
-    lax.fori_loop(0, ROWS // UNROLL, scatter, 0)
-    chunk = FLAT // 4
-    copies = [
-        pltpu.make_async_copy(
-            out_v.at[pl.ds(i * chunk, chunk)], out.at[pl.ds(i * chunk, chunk)], out_sem.at[i]
-        )
-        for i in range(4)
-    ]
-    for c in copies:
-        c.start()
+            out4[t : t + 32, c] = turned4[t : t + 32, c] + block[:, c * 128 : (c + 1) * 128].reshape(32, 8, 128)
+        rows = pl.ds(i * (FLAT // 8), FLAT // 8)
+        copies.append(pltpu.make_async_copy(out_v.at[rows], out.at[rows], out_sem.at[i]))
+        copies[-1].start()
     for c in copies:
         c.wait()
 
@@ -387,19 +437,21 @@
     flat_points = points.reshape(TILES, 8, LANES, 128).transpose(0, 2, 1, 3).reshape(FLAT, 128)
     order_rows = order.reshape(ROWS // 128, 128)
     vmem = pl.BlockSpec(memory_space=pltpu.VMEM)
-    smem = pl.BlockSpec(memory_space=pltpu.SMEM)
     hbm = pl.BlockSpec(memory_space=pltpu.HBM)
     dma = pltpu.SemaphoreType.DMA
-    acc, low0 = pl.pallas_call(
+    turned, turned_basis, low0 = pl.pallas_call(
         tree_kernel,
         out_shape=(
-            jax.ShapeDtypeStruct((FLAT, 128), F32),
-            jax.ShapeDtypeStruct((2, COLS, RANK), BF16),
+            pltpu.VMEM((2 * FLAT, 128), F32),
+            pltpu.VMEM((ROWS, COLS), BF16),
+            pltpu.VMEM((COLS, 2 * RANK), BF16),
         ),
-        in_specs=[vmem, smem] + [hbm] * 7,
-        out_specs=(vmem, vmem),
+        in_specs=[hbm] * 10,
+        out_specs=(vmem, vmem, vmem),
         scratch_shapes=[
             pltpu.VMEM((FLAT, 128), F32),
+            pltpu.VMEM((2 * FLAT, 128), F32),
+            pltpu.VMEM((2, LEAF, RANK), BF16),
             pltpu.VMEM((2, LEAF, LEAF), BF16),
             pltpu.VMEM((2, LEAF, RANK), BF16),
             pltpu.VMEM((2, 3, RANK, RANK), BF16),
@@ -408,6 +460,10 @@
             pltpu.VMEM((RANK, RANK), BF16),
             pltpu.VMEM((RANK, RANK), BF16),
             pltpu.VMEM((3, 3, RANK, RANK), BF16),
+            pltpu.VMEM((ROWS // 128, 128), jnp.int32),
+            pltpu.SMEM((1,), F32),
+            pltpu.VMEM((ROWS // 128, 128), jnp.int32),
+            pltpu.SMEM((ROWS // 128, 128), jnp.int32),
             pltpu.VMEM((ROWS // 128, 128), jnp.int32),
             pltpu.SMEM((ROWS // 128, 128), jnp.int32),
             pltpu.VMEM((ROWS, COLS), BF16),
@@ -423,26 +479,27 @@
             pltpu.VMEM((HALF, RANK), F32),
             pltpu.VMEM((4 * PART, RANK), BF16),
             pltpu.VMEM((COLS, RANK), BF16),
-            dma((8,)),
+            dma((2,)),
+            dma((9,)),
             dma((4,)),
-            dma,
             dma((2,)),
             dma((2,)),
-            dma((3,)),
-            dma((3,)),
-            dma((3,)),
-            dma((3,)),
-            dma((3,)),
-            dma((3,)),
-            dma((3,)),
-            dma((3,)),
-            dma((3,)),
-            dma((3,)),
-            dma,
-            dma,
+            dma((2,)),
+            dma((3,)),
+            dma((3,)),
+            dma((3,)),
+            dma((3,)),
+            dma((3,)),
+            dma((3,)),
+            dma((3,)),
+            dma((3,)),
+            dma((3,)),
+            dma((3,)),
+            dma((4,)),
+            dma((4,)),
         ],
         compiler_params=pltpu.CompilerParams(
-            collective_id=0, has_side_effects=True, vmem_limit_bytes=54 << 20
+            collective_id=0, has_side_effects=True, vmem_limit_bytes=44 << 20
         ),
         name="tree",
     )(
@@ -451,6 +508,7 @@
         flat_points,
         near,
         basis_in,
+        basis_out,
         leaf_coupling,
         transfer_up,
         transfer_down,
@@ -459,19 +517,12 @@
     out = pl.pallas_call(
         leaf_kernel,
         out_shape=jax.ShapeDtypeStruct((FLAT, 128), F32),
-        in_specs=[vmem] * 4,
+        in_specs=[vmem] * 3,
         out_specs=hbm,
-        scratch_shapes=[
-            pltpu.VMEM((ROWS // 128, 128), jnp.int32),
-            pltpu.SMEM((ROWS // 128, 128), jnp.int32),
-            pltpu.VMEM((FLAT, 128), F32),
-            pltpu.VMEM((FLAT, 128), F32),
-            dma,
-            dma((4,)),
-        ],
-        compiler_params=pltpu.CompilerParams(vmem_limit_bytes=24 << 20),
+        scratch_shapes=[pltpu.VMEM((FLAT, 128), F32), dma((8,))],
+        compiler_params=pltpu.CompilerParams(vmem_limit_bytes=12 << 20),
         name="leaves",
-    )(order_rows, acc, basis_out, low0)
+    )(turned, turned_basis, low0)
     return out.reshape(TILES, LANES, 8, 128).transpose(0, 2, 1, 3).reshape(ROWS, COLS)
 
 

time: 48.8 us -> 37.1 us (0.76)
  Pallas kernels: 44.7 us -> 36.4 us
  local copies, waits for them, and re-layouts: 3.23 us -> 0 us
    pallas_call x1, Pallas kernels: 7.88 us -> 2.41 us  [on_device(): pl.pallas_call(leaf_kernel, out_shape=jax.ShapeDtypeStruct((FLAT, 128), F...]
    unnamed x8 -> x0, local copies, waits for them, and re-layouts: 3.23 us -> none
    pallas_call x1, Pallas kernels: 36.8 us -> 33.9 us  [on_device(): pl.pallas_call(tree_kernel, out_shape=(pltpu.VMEM((2 * FLAT, 128), F32),...]
where the time goes in v2:
time: 37.1 us; the launch traced here: 37 us
  Pallas kernels  36.4 us (98%)
  between operations  0.66 us (2%)
    pallas_call x1, Pallas kernels, on_device(): pl.pallas_call(tree_kernel, out_shape=(pltpu.VMEM((2 * FLAT, 128), F32),...  33.9 us
    pallas_call x1, Pallas kernels, on_device(): pl.pallas_call(leaf_kernel, out_shape=jax.ShapeDtypeStruct((FLAT, 128), F...  2.41 us

profile of v2, /device:TPU:1, one launch (start us, length us, event | category | flops | bytes accessed | tf_op | source)
XLA Modules:
  0.0 37.0 jit_solution(2003378788444559810)
XLA Ops:
  0.7 33.9 %tree.1 = (f32[16384,128]{1,0:T(8,128)S(1)}, bf16[2048,512]{1,0:T(8,128)(2,1)S(1)}, bf16[512,512]{1,0:T(8,128)(2,1)S(1)}) custom-call(s32[16,128]{1,0:T(8,128)} %bitcast.12, f32[1]{0:T(128)S(6)} %copy.11.ridge, f32[8192,128]{1,0:T(8,128)} %bitcast.11, bf16[2,1024,1024]{2,1,0:T(8,128)(2,1)} %near.1, bf16[2,1024,256]{2,1,0:T(8,128)(2,1)} %basis_in.1, ...), custom_call_target="tpu_custom_call" | custom-call | tf_op jit(solution)/shard_map/tree/pallas_call | solution.py:442
  34.6 2.4 %leaves.1 = f32[8192,128]{1,0:T(8,128)} custom-call(f32[16384,128]{1,0:T(8,128)S(1)} %get-tuple-element.8.turned, bf16[2048,512]{1,0:T(8,128)(2,1)S(1)} %get-tuple-element.9.turned_basis, bf16[512,512]{1,0:T(8,128)(2,1)S(1)} %get-tuple-element.10.low0), custom_call_target="tpu_custom_call" | custom-call | tf_op jit(solution)/shard_map/leaves/pallas_call | solution.py:517

commit v3 on v2

--- a/solution.py
+++ b/solution.py
@@ -141,6 +141,12 @@
     for dev in [twin] + on_x[1:] + on_y[1:] + on_g[1:]:
         pl.semaphore_signal(barrier, inc=1, device_id=dev, device_id_type=MESH)
 
+    small = [
+        pltpu.make_async_copy(order, order_v, small_sem.at[0]),
+        pltpu.make_async_copy(ridge, ridge_s, small_sem.at[1]),
+    ]
+    for c in small:
+        c.start()
     chunk = FLAT // 4
     point_copies = [
         pltpu.make_async_copy(
@@ -152,20 +158,11 @@
     ]
     for c in point_copies:
         c.start()
-    small = [
-        pltpu.make_async_copy(order, order_v, small_sem.at[0]),
-        pltpu.make_async_copy(ridge, ridge_s, small_sem.at[1]),
-    ]
-    for c in small:
-        c.start()
     small[0].wait()
     local = order_v[...] & (ROWS - 1)
     place_v[...] = row_places(local, LANES)
     place_copy = pltpu.make_async_copy(place_v, place_s, place_sem.at[0])
     place_copy.start()
-    back_v[...] = row_places(inverse_of(local), WIDE)
-    back_copy = pltpu.make_async_copy(back_v, back_s, place_sem.at[1])
-    back_copy.start()
 
     def rank_rows(i):
         return pl.ds(pl.multiple_of(i * RANK, RANK), RANK)
@@ -232,7 +229,6 @@
 
     small[1].wait()
     gain = ridge_s[0]
-    loads[2].wait()
 
     def near_chunk(i):
         leaf, q = i // 4, i % 4
@@ -266,8 +262,6 @@
 
     loads[1].wait()
     total1 = nn(hat0[0, mine], up_v[0, rank_rows(2 * k)]) + nn(hat0[1, mine], up_v[0, rank_rows(2 * k + 1)])
-    near_chunk(0)
-    near_chunk(1)
     remote(hat0.at[:, other], sib0.at[:, mine], a_send.at[0], a_recv.at[0], twin).wait_recv()
     sib = 1 - k
     total1 += nn(sib0[0, mine], up_v[0, rank_rows(2 * sib)]) + nn(sib0[1, mine], up_v[0, rank_rows(2 * sib + 1)])
@@ -297,11 +291,13 @@
         )
     for j in (2, 1, 3):
         b_copies[j].start()
-    for j in (2, 1, 3):
-        b2_copies[j].start()
 
     total2 = nn(hat1[pl.ds(pl.multiple_of(x * PART, PART), PART)], up_v[1, rank_rows(x)])
-    for i in range(2, 8):
+    back_v[...] = row_places(inverse_of(local), WIDE)
+    back_copy = pltpu.make_async_copy(back_v, back_s, place_sem.at[1])
+    back_copy.start()
+    loads[2].wait()
+    for i in range(0, 8):
         near_chunk(i)
     loads[8].wait()
     basis_rows(0)
@@ -317,6 +313,8 @@
     ]
     for j in (2, 1, 3):
         c_copies[j].start()
+    for j in (2, 1, 3):
+        b2_copies[j].start()
 
     total3 = nn(hat2[...], up_v[2, rank_rows(gy)])
     turn(0, 7)

time: 37.1 us -> 35.1 us (0.946)
  Pallas kernels: 36.4 us -> 34.3 us
    pallas_call x1, Pallas kernels: 33.9 us -> 31.9 us  [on_device(): pl.pallas_call(tree_kernel, out_shape=(pltpu.VMEM((2 * FLAT, 128), F32),...]
where the time goes in v3:
time: 35.1 us; the launch traced here: 34.9 us
  Pallas kernels  34.3 us (98%)
  between operations  0.66 us (2%)
    pallas_call x1, Pallas kernels, on_device(): pl.pallas_call(tree_kernel, out_shape=(pltpu.VMEM((2 * FLAT, 128), F32),...  31.9 us
    pallas_call x1, Pallas kernels, on_device(): pl.pallas_call(leaf_kernel, out_shape=jax.ShapeDtypeStruct((FLAT, 128), F...  2.41 us

profile of v3, /device:TPU:1, one launch (start us, length us, event | category | flops | bytes accessed | tf_op | source)
XLA Modules:
  0.0 34.9 jit_solution(2377247753888588586)
XLA Ops:
  0.7 31.9 %tree.1 = (f32[16384,128]{1,0:T(8,128)S(1)}, bf16[2048,512]{1,0:T(8,128)(2,1)S(1)}, bf16[512,512]{1,0:T(8,128)(2,1)S(1)}) custom-call(s32[16,128]{1,0:T(8,128)} %bitcast.12, f32[1]{0:T(128)S(6)} %copy.11.ridge, f32[8192,128]{1,0:T(8,128)} %bitcast.11, bf16[2,1024,1024]{2,1,0:T(8,128)(2,1)} %near.1, bf16[2,1024,256]{2,1,0:T(8,128)(2,1)} %basis_in.1, ...), custom_call_target="tpu_custom_call" | custom-call | tf_op jit(solution)/shard_map/tree/pallas_call | solution.py:440
  32.5 2.4 %leaves.1 = f32[8192,128]{1,0:T(8,128)} custom-call(f32[16384,128]{1,0:T(8,128)S(1)} %get-tuple-element.8.turned, bf16[2048,512]{1,0:T(8,128)(2,1)S(1)} %get-tuple-element.9.turned_basis, bf16[512,512]{1,0:T(8,128)(2,1)S(1)} %get-tuple-element.10.low0), custom_call_target="tpu_custom_call" | custom-call | tf_op jit(solution)/shard_map/leaves/pallas_call | solution.py:515

commit v4 on v3

--- a/solution.py
+++ b/solution.py
@@ -15,6 +15,7 @@
 RANK = 256
 HALF = 256
 PART = 64
+BITE = PART // 2
 TILES = ROWS // 8
 LANES = COLS // 128
 FLAT = ROWS * LANES
@@ -22,6 +23,7 @@
 GROUP = 128
 GROUPS = ROWS // GROUP
 BATCH = 16
+B_NEAR, C_TURN, D_TURN = 5, 4, 6
 
 
 def nt(a, b):
@@ -66,7 +68,6 @@
 
 def tree_kernel(
     order,
-    ridge,
     points,
     near,
     basis_in,
@@ -90,7 +91,6 @@
     dn3_v,
     nc_v,
     order_v,
-    ridge_s,
     place_v,
     place_s,
     back_v,
@@ -108,7 +108,7 @@
     far1,
     low2,
     low1,
-    small_sem,
+    order_sem,
     load_sem,
     point_sem,
     place_sem,
@@ -137,16 +137,8 @@
     on_y = [None] + [(gx, lax.rem(gy + j, 4), gz) for j in (1, 2, 3)]
     on_g = [None] + [(lax.rem(gx + j, 4), gy, gz) for j in (1, 2, 3)]
 
-    barrier = pltpu.get_barrier_semaphore()
-    for dev in [twin] + on_x[1:] + on_y[1:] + on_g[1:]:
-        pl.semaphore_signal(barrier, inc=1, device_id=dev, device_id_type=MESH)
-
-    small = [
-        pltpu.make_async_copy(order, order_v, small_sem.at[0]),
-        pltpu.make_async_copy(ridge, ridge_s, small_sem.at[1]),
-    ]
-    for c in small:
-        c.start()
+    order_copy = pltpu.make_async_copy(order, order_v, order_sem)
+    order_copy.start()
     chunk = FLAT // 4
     point_copies = [
         pltpu.make_async_copy(
@@ -158,7 +150,11 @@
     ]
     for c in point_copies:
         c.start()
-    small[0].wait()
+    barrier = pltpu.get_barrier_semaphore()
+    for dev in [twin] + on_x[1:] + on_y[1:] + on_g[1:]:
+        pl.semaphore_signal(barrier, inc=1, device_id=dev, device_id_type=MESH)
+
+    order_copy.wait()
     local = order_v[...] & (ROWS - 1)
     place_v[...] = row_places(local, LANES)
     place_copy = pltpu.make_async_copy(place_v, place_s, place_sem.at[0])
@@ -208,34 +204,34 @@
             src_ref=src, dst_ref=dst, send_sem=send, recv_sem=recv, device_id=dev, device_id_type=MESH
         )
 
-    def leaf_up(columns):
-        for leaf in range(2):
-            hat0[leaf, columns] = lax.dot_general(
-                rounded[leaf * LEAF : (leaf + 1) * LEAF, columns],
-                basis_v[leaf],
-                (((0,), (0,)), ((), ())),
-                preferred_element_type=F32,
-            ).astype(BF16)
+    def leaf_up(leaf, columns):
+        hat0[leaf, columns] = lax.dot_general(
+            rounded[leaf * LEAF : (leaf + 1) * LEAF, columns],
+            basis_v[leaf],
+            (((0,), (0,)), ((), ())),
+            preferred_element_type=F32,
+        ).astype(BF16)
 
     a_copies = [
-        remote(hat0.at[:, rows], sib0.at[:, rows], a_send.at[i], a_recv.at[i], twin)
-        for i, rows in enumerate((other, mine))
+        remote(hat0.at[0, other], sib0.at[0, other], a_send.at[0], a_recv.at[0], twin),
+        remote(hat0.at[1, other], sib0.at[1, other], a_send.at[1], a_recv.at[1], twin),
+        remote(hat0.at[:, mine], sib0.at[:, mine], a_send.at[2], a_recv.at[2], twin),
     ]
-    leaf_up(other)
+    leaf_up(0, other)
     pl.semaphore_wait(barrier, 10)
     a_copies[0].start()
-    leaf_up(mine)
+    leaf_up(1, other)
     a_copies[1].start()
-
-    small[1].wait()
-    gain = ridge_s[0]
+    leaf_up(0, mine)
+    leaf_up(1, mine)
+    a_copies[2].start()
 
     def near_chunk(i):
         leaf, q = i // 4, i % 4
         block = nn(near_v[leaf, q * 256 : (q + 1) * 256], rounded[leaf * LEAF : (leaf + 1) * LEAF])
         t = leaf * 128 + q * 32
         for c in range(LANES):
-            wide4[t : t + 32, c] = wide4[t : t + 32, c] * gain + block[:, c * 128 : (c + 1) * 128].reshape(32, 8, 128)
+            wide4[t : t + 32, c] = block[:, c * 128 : (c + 1) * 128].reshape(32, 8, 128)
 
     def basis_rows(leaf):
         none = jnp.zeros((32, 8, 128), F32)
@@ -260,11 +256,41 @@
 
         lax.fori_loop(first, first + count, step, 0)
 
+    def bites(kind):
+        return [kind[j][h] for h in (0, 1) for j in (2, 1, 3)]
+
+    def skip(s, own):
+        return jnp.where(s > own, s - 1, s)
+
+    def before(own, j):
+        return lax.rem(own - j + 4, 4)
+
+    def spread(source, target, send, recv, where):
+        return [None] + [
+            [
+                remote(
+                    source.at[h * BITE : (h + 1) * BITE],
+                    target.at[h * BITE : (h + 1) * BITE],
+                    send.at[j - 1, h],
+                    recv.at[j - 1, h],
+                    where[j],
+                )
+                for h in (0, 1)
+            ]
+            for j in (1, 2, 3)
+        ]
+
     loads[1].wait()
     total1 = nn(hat0[0, mine], up_v[0, rank_rows(2 * k)]) + nn(hat0[1, mine], up_v[0, rank_rows(2 * k + 1)])
-    remote(hat0.at[:, other], sib0.at[:, mine], a_send.at[0], a_recv.at[0], twin).wait_recv()
+    back_v[...] = row_places(inverse_of(local), WIDE)
+    back_copy = pltpu.make_async_copy(back_v, back_s, place_sem.at[1])
+    back_copy.start()
     sib = 1 - k
-    total1 += nn(sib0[0, mine], up_v[0, rank_rows(2 * sib)]) + nn(sib0[1, mine], up_v[0, rank_rows(2 * sib + 1)])
+    for leaf in range(2):
+        remote(
+            hat0.at[leaf, other], sib0.at[leaf, mine], a_send.at[leaf], a_recv.at[leaf], twin
+        ).wait_recv()
+        total1 += nn(sib0[leaf, mine], up_v[0, rank_rows(2 * sib + leaf)])
     value1 = total1.astype(BF16)
     hat1[0:HALF] = value1
     hat1[HALF : 2 * HALF] = value1
@@ -272,13 +298,16 @@
     for j in (1, 2, 3):
         start = lax.rem(x + j, 4) * PART
         b_copies.append(
-            remote(
-                hat1.at[pl.ds(pl.multiple_of(start, PART), PART)],
-                all1.at[x, 0:PART],
-                b_send.at[j - 1],
-                b_recv.at[j - 1],
-                on_x[j],
-            )
+            [
+                remote(
+                    hat1.at[pl.ds(pl.multiple_of(start + h * BITE, BITE), BITE)],
+                    all1.at[x, h * BITE : (h + 1) * BITE],
+                    b_send.at[j - 1, h],
+                    b_recv.at[j - 1, h],
+                    on_x[j],
+                )
+                for h in (0, 1)
+            ]
         )
         b2_copies.append(
             remote(
@@ -289,102 +318,114 @@
                 on_x[j],
             )
         )
+    for c in bites(b_copies):
+        c.start()
+
+    total2 = nn(hat1[pl.ds(pl.multiple_of(x * PART, PART), PART)], up_v[1, rank_rows(x)])
+    loads[2].wait()
+    for i in range(B_NEAR):
+        near_chunk(i)
+    c_copies = spread(hat2, all2.at[gy], c_send, c_recv, on_y)
+    for h in (0, 1):
+        rows = slice(h * BITE, (h + 1) * BITE)
+        part = total2[rows]
+        for j in (1, 3, 2):
+            s = before(x, j)
+            b_copies[j][h].wait_recv()
+            part += nn(all1[s, rows], up_v[1, rank_rows(s)])
+        hat2[rows] = part.astype(BF16)
+        for j in (2, 1, 3):
+            c_copies[j][h].start()
     for j in (2, 1, 3):
-        b_copies[j].start()
-
-    total2 = nn(hat1[pl.ds(pl.multiple_of(x * PART, PART), PART)], up_v[1, rank_rows(x)])
-    back_v[...] = row_places(inverse_of(local), WIDE)
-    back_copy = pltpu.make_async_copy(back_v, back_s, place_sem.at[1])
-    back_copy.start()
-    loads[2].wait()
-    for i in range(0, 8):
+        b2_copies[j].start()
+
+    total3 = nn(hat2[...], up_v[2, rank_rows(gy)])
+    for i in range(B_NEAR, 8):
         near_chunk(i)
     loads[8].wait()
     basis_rows(0)
     basis_rows(1)
     back_copy.wait()
-    for j in (1, 3, 2):
-        s = lax.rem(x - j + 4, 4)
-        b_copies[j].wait_recv()
-        total2 += nn(all1[s, 0:PART], up_v[1, rank_rows(s)])
-    hat2[...] = total2.astype(BF16)
-    c_copies = [None] + [
-        remote(hat2, all2.at[gy], c_send.at[j - 1], c_recv.at[j - 1], on_y[j]) for j in (1, 2, 3)
-    ]
-    for j in (2, 1, 3):
-        c_copies[j].start()
-    for j in (2, 1, 3):
-        b2_copies[j].start()
-
-    total3 = nn(hat2[...], up_v[2, rank_rows(gy)])
-    turn(0, 7)
-    for j in (1, 3, 2):
-        s = lax.rem(gy - j + 4, 4)
-        c_copies[j].wait_recv()
-        total3 += nn(all2[s], up_v[2, rank_rows(s)])
-    hat3[...] = total3.astype(BF16)
-    d_copies = [None] + [
-        remote(hat3, all3.at[gx], d_send.at[j - 1], d_recv.at[j - 1], on_g[j]) for j in (1, 2, 3)
-    ]
-    for j in (2, 1, 3):
-        d_copies[j].start()
-
-    def skip(s, own):
-        return jnp.where(s > own, s - 1, s)
+    turn(0, C_TURN)
+    d_copies = spread(hat3, all3.at[gx], d_send, d_recv, on_g)
+    for h in (0, 1):
+        rows = slice(h * BITE, (h + 1) * BITE)
+        part = total3[rows]
+        for j in (1, 3, 2):
+            s = before(gy, j)
+            c_copies[j][h].wait_recv()
+            part += nn(all2[s, rows], up_v[2, rank_rows(s)])
+        hat3[rows] = part.astype(BF16)
+        for j in (2, 1, 3):
+            d_copies[j][h].start()
 
     loads[3].wait()
     loads[4].wait()
     far2 = jnp.zeros((PART, RANK), F32)
     for j in (1, 2, 3):
-        s = lax.rem(gy - j + 4, 4)
+        s = before(gy, j)
         far2 += nt(all2[s], nc_v[1, skip(s, gy)])
-    a_copies[1].wait_recv()
+    a_copies[2].wait_recv()
     for leaf in range(2):
         far0[leaf] = (
             nt(hat0[1 - leaf], lc_v[leaf, 2 * k])
             + nt(sib0[0], lc_v[leaf, 1 - k])
             + nt(sib0[1], lc_v[leaf, 2 - k])
         )
-    turn(7, 3)
-    far3 = jnp.zeros((PART, RANK), F32)
-    for j in (1, 3, 2):
-        s = lax.rem(gx - j + 4, 4)
-        d_copies[j].wait_recv()
-        far3 += nt(all3[s], nc_v[2, skip(s, gx)])
-
+    turn(C_TURN, D_TURN)
     loads[7].wait()
-    value2 = (far2 + nt(far3.astype(BF16), dn3_v[...])).astype(BF16)
-    low2[0:PART] = value2
+
     e_copies = [None] + [
-        remote(
-            low2.at[0:PART],
-            low2.at[(4 - j) * PART : (5 - j) * PART],
-            e_send.at[j - 1],
-            e_recv.at[j - 1],
-            on_x[j],
-        )
+        [
+            remote(
+                low2.at[h * BITE : (h + 1) * BITE],
+                low2.at[(4 - j) * PART + h * BITE : (4 - j) * PART + (h + 1) * BITE],
+                e_send.at[j - 1, h],
+                e_recv.at[j - 1, h],
+                on_x[j],
+            )
+            for h in (0, 1)
+        ]
         for j in (1, 2, 3)
     ]
-    for j in (2, 1, 3):
-        e_copies[j].start()
+    for h in (0, 1):
+        rows = slice(h * BITE, (h + 1) * BITE)
+        far3 = jnp.zeros((BITE, RANK), F32)
+        for j in (1, 3, 2):
+            s = before(gx, j)
+            d_copies[j][h].wait_recv()
+            far3 += nt(all3[s, rows], nc_v[2, skip(s, gx)])
+        low2[rows] = (far2[rows] + nt(far3.astype(BF16), dn3_v[...])).astype(BF16)
+        for j in (2, 1, 3):
+            e_copies[j][h].start()
     total = jnp.zeros((HALF, RANK), F32)
     for j in (1, 2, 3):
-        s = lax.rem(x - j + 4, 4)
+        s = before(x, j)
         b2_copies[j].wait_recv()
         total += nt(all1[s], nc_v[0, skip(s, x)])
     far1[...] = total
-    turn(10, 6)
+    turn(C_TURN + D_TURN, GROUPS - C_TURN - D_TURN)
+    turned_to_bf16(0, GROUPS)
     loads[6].wait()
     f_copies = []
-    for m in (0, 3, 1, 2):
+
+    def half_rows(core, m, first):
+        return core * HALF + lax.rem(x + m, 4) * PART + first
+
+    def low1_block(m, first, count):
+        at = m * PART + first
+        value = far1[at : at + count] + nt(low2[at : at + count], dn2_v[...])
+        rows = pl.ds(pl.multiple_of(half_rows(k, m, first), BITE), count)
+        low1[rows] = value.astype(BF16)
+        n = len(f_copies)
+        f_copies.append(remote(low1.at[rows], low1.at[rows], f_send.at[n], f_recv.at[n], twin))
+        f_copies[-1].start()
+
+    blocks = [(0, 0, PART)] + [(m, h * BITE, BITE) for h in (0, 1) for m in (3, 1, 2)]
+    for m, first, count in blocks:
         if m:
-            e_copies[4 - m].wait_recv()
-        value = far1[m * PART : (m + 1) * PART] + nt(low2[m * PART : (m + 1) * PART], dn2_v[...])
-        to = k * HALF + lax.rem(x + m, 4) * PART
-        rows = pl.ds(pl.multiple_of(to, PART), PART)
-        low1[rows] = value.astype(BF16)
-        f_copies.append(remote(low1.at[rows], low1.at[rows], f_send.at[m], f_recv.at[m], twin))
-        f_copies[-1].start()
+            e_copies[4 - m][first // BITE].wait_recv()
+        low1_block(m, first, count)
     loads[5].wait()
 
     def leaf_down(rows):
@@ -393,18 +434,21 @@
             low0[rows, leaf * RANK : (leaf + 1) * RANK] = value.astype(BF16)
 
     leaf_down(mine)
-    turned_to_bf16(0, 16)
-    for m in (0, 3, 1, 2):
-        to = (1 - k) * HALF + lax.rem(x + m, 4) * PART
-        rows = pl.ds(pl.multiple_of(to, PART), PART)
-        remote(low1.at[rows], low1.at[rows], f_send.at[m], f_recv.at[m], twin).wait_recv()
+    for n, (m, first, count) in enumerate(blocks):
+        rows = pl.ds(pl.multiple_of(half_rows(1 - k, m, first), BITE), count)
+        remote(low1.at[rows], low1.at[rows], f_send.at[n], f_recv.at[n], twin).wait_recv()
     leaf_down(other)
 
-    for c in a_copies + b_copies[1:] + b2_copies[1:] + c_copies[1:] + d_copies[1:] + e_copies[1:] + f_copies:
+    for c in a_copies + b2_copies[1:] + f_copies:
         c.wait_send()
-
-
-def leaf_kernel(turned, turned_basis, low0, out, out_v, out_sem):
+    for kind in (b_copies, c_copies, d_copies, e_copies):
+        for c in bites(kind):
+            c.wait_send()
+
+
+def leaf_kernel(ridge, turned, turned_basis, low0, points, out, out_v, out_sem):
+    gain = ridge[0]
+    points4 = points.reshape(TILES, LANES, 8, 128)
     turned4 = turned.reshape(TILES, WIDE, 8, 128)
     out4 = out_v.reshape(TILES, LANES, 8, 128)
     copies = []
@@ -412,7 +456,8 @@
         block = nt(turned_basis[i * 256 : (i + 1) * 256], low0[...])
         t = i * 32
         for c in range(LANES):
-            out4[t : t + 32, c] = turned4[t : t + 32, c] + block[:, c * 128 : (c + 1) * 128].reshape(32, 8, 128)
+            fixed = turned4[t : t + 32, c] + points4[t : t + 32, c] * gain
+            out4[t : t + 32, c] = fixed + block[:, c * 128 : (c + 1) * 128].reshape(32, 8, 128)
         rows = pl.ds(i * (FLAT // 8), FLAT // 8)
         copies.append(pltpu.make_async_copy(out_v.at[rows], out.at[rows], out_sem.at[i]))
         copies[-1].start()
@@ -437,17 +482,17 @@
     vmem = pl.BlockSpec(memory_space=pltpu.VMEM)
     hbm = pl.BlockSpec(memory_space=pltpu.HBM)
     dma = pltpu.SemaphoreType.DMA
-    turned, turned_basis, low0 = pl.pallas_call(
+    turned, turned_basis, low0, held_points = pl.pallas_call(
         tree_kernel,
         out_shape=(
             pltpu.VMEM((2 * FLAT, 128), F32),
             pltpu.VMEM((ROWS, COLS), BF16),
             pltpu.VMEM((COLS, 2 * RANK), BF16),
+            pltpu.VMEM((FLAT, 128), F32),
         ),
-        in_specs=[hbm] * 10,
-        out_specs=(vmem, vmem, vmem),
+        in_specs=[hbm] * 9,
+        out_specs=(vmem, vmem, vmem, vmem),
         scratch_shapes=[
-            pltpu.VMEM((FLAT, 128), F32),
             pltpu.VMEM((2 * FLAT, 128), F32),
             pltpu.VMEM((2, LEAF, RANK), BF16),
             pltpu.VMEM((2, LEAF, LEAF), BF16),
@@ -459,7 +504,6 @@
             pltpu.VMEM((RANK, RANK), BF16),
             pltpu.VMEM((3, 3, RANK, RANK), BF16),
             pltpu.VMEM((ROWS // 128, 128), jnp.int32),
-            pltpu.SMEM((1,), F32),
             pltpu.VMEM((ROWS // 128, 128), jnp.int32),
             pltpu.SMEM((ROWS // 128, 128), jnp.int32),
             pltpu.VMEM((ROWS // 128, 128), jnp.int32),
@@ -477,32 +521,31 @@
             pltpu.VMEM((HALF, RANK), F32),
             pltpu.VMEM((4 * PART, RANK), BF16),
             pltpu.VMEM((COLS, RANK), BF16),
-            dma((2,)),
+            dma,
             dma((9,)),
             dma((4,)),
             dma((2,)),
-            dma((2,)),
-            dma((2,)),
             dma((3,)),
             dma((3,)),
+            dma((3, 2)),
+            dma((3, 2)),
             dma((3,)),
             dma((3,)),
-            dma((3,)),
-            dma((3,)),
-            dma((3,)),
-            dma((3,)),
-            dma((3,)),
-            dma((3,)),
-            dma((4,)),
-            dma((4,)),
+            dma((3, 2)),
+            dma((3, 2)),
+            dma((3, 2)),
+            dma((3, 2)),
+            dma((3, 2)),
+            dma((3, 2)),
+            dma((7,)),
+            dma((7,)),
         ],
         compiler_params=pltpu.CompilerParams(
-            collective_id=0, has_side_effects=True, vmem_limit_bytes=44 << 20
+            collective_id=0, has_side_effects=True, vmem_limit_bytes=40 << 20
         ),
         name="tree",
     )(
         order_rows,
-        ridge,
         flat_points,
         near,
         basis_in,
@@ -515,12 +558,12 @@
     out = pl.pallas_call(
         leaf_kernel,
         out_shape=jax.ShapeDtypeStruct((FLAT, 128), F32),
-        in_specs=[vmem] * 3,
+        in_specs=[pl.BlockSpec(memory_space=pltpu.SMEM)] + [vmem] * 4,
         out_specs=hbm,
         scratch_shapes=[pltpu.VMEM((FLAT, 128), F32), dma((8,))],
         compiler_params=pltpu.CompilerParams(vmem_limit_bytes=12 << 20),
         name="leaves",
-    )(turned, turned_basis, low0)
+    )(ridge, turned, turned_basis, low0, held_points)
     return out.reshape(TILES, LANES, 8, 128).transpose(0, 2, 1, 3).reshape(ROWS, COLS)
 
 

time: 35.1 us -> 33.9 us (0.966)
  Pallas kernels: 34.3 us -> 33.1 us
    pallas_call x1, Pallas kernels: 31.9 us -> 30.7 us  [on_device(): pl.pallas_call(tree_kernel, out_shape=(pltpu.VMEM((2 * FLAT, 128), F32),...]
where the time goes in v4:
time: 33.9 us; the launch traced here: 33.8 us
  Pallas kernels  33.1 us (98%)
  between operations  0.66 us (2%)
    pallas_call x1, Pallas kernels, on_device(): pl.pallas_call(tree_kernel, out_shape=(pltpu.VMEM((2 * FLAT, 128), F32),...  30.7 us
    pallas_call x1, Pallas kernels, on_device(): pl.pallas_call(leaf_kernel, out_shape=jax.ShapeDtypeStruct((FLAT, 128), F...  2.4 us

profile of v4, /device:TPU:1, one launch (start us, length us, event | category | flops | bytes accessed | tf_op | source)
XLA Modules:
  0.0 33.8 jit_solution(15061203135921703410)
XLA Ops:
  0.7 30.7 %tree.1 = (f32[16384,128]{1,0:T(8,128)S(1)}, bf16[2048,512]{1,0:T(8,128)(2,1)S(1)}, bf16[512,512]{1,0:T(8,128)(2,1)S(1)}, f32[8192,128]{1,0:T(8,128)S(1)}) custom-call(s32[16,128]{1,0:T(8,128)} %bitcast.12, f32[8192,128]{1,0:T(8,128)} %bitcast.11, bf16[2,1024,1024]{2,1,0:T(8,128)(2,1)} %near.1, bf16[2,1024,256]{2,1,0:T(8,128)(2,1)} %basis_in.1, ...), custom_call_target="tpu_custom_call" | custom-call | tf_op jit(solution)/shard_map/tree/pallas_call | solution.py:485
  31.4 2.4 %leaves.1 = f32[8192,128]{1,0:T(8,128)} custom-call(f32[1]{0:T(128)S(6)} %copy.11.ridge, f32[16384,128]{1,0:T(8,128)S(1)} %get-tuple-element.9.turned, bf16[2048,512]{1,0:T(8,128)(2,1)S(1)} %get-tuple-element.10.turned_basis, bf16[512,512]{1,0:T(8,128)(2,1)S(1)} %get-tuple-element.11.low0, f32[8192,128]{1,0:T(8,128)S(1)} %get-tuple-element.12.points), custom_call_target="tpu_custom_call" | custom-call | tf_op jit(solution)/shard_map/leaves/pallas_call | solution.py:558

commit v5 on v4

--- a/solution.py
+++ b/solution.py
@@ -187,13 +187,18 @@
     move_rows(place_s, pts_v, wide, LANES, WIDE, 0, GROUPS)
     wide4 = wide.reshape(TILES, WIDE, 8, 128)
 
-    def to_bf16(step, _):
-        for c in range(LANES):
-            block = wide4[pl.ds(step * 16, 16), c]
-            rounded[pl.ds(step * 128, 128), c * 128 : (c + 1) * 128] = block.reshape(128, 128).astype(BF16)
-        return 0
-
-    lax.fori_loop(0, ROWS // 128, to_bf16, 0)
+    def to_bf16(core):
+        def step(i, _):
+            for tile in range(LANES // 2):
+                c = core * (LANES // 2) + tile
+                block = wide4[pl.ds(i * 32, 32), c]
+                lanes = pl.ds(pl.multiple_of(c * 128, 128), 128)
+                rounded[pl.ds(i * 256, 256), lanes] = block.reshape(256, 128).astype(BF16)
+            return 0
+
+        lax.fori_loop(0, ROWS // 256, step, 0)
+
+    to_bf16(1 - k)
 
     loads[0].wait()
     mine = pl.ds(pl.multiple_of(k * HALF, HALF), HALF)
@@ -222,6 +227,7 @@
     a_copies[0].start()
     leaf_up(1, other)
     a_copies[1].start()
+    to_bf16(k)
     leaf_up(0, mine)
     leaf_up(1, mine)
     a_copies[2].start()
@@ -282,9 +288,6 @@
 
     loads[1].wait()
     total1 = nn(hat0[0, mine], up_v[0, rank_rows(2 * k)]) + nn(hat0[1, mine], up_v[0, rank_rows(2 * k + 1)])
-    back_v[...] = row_places(inverse_of(local), WIDE)
-    back_copy = pltpu.make_async_copy(back_v, back_s, place_sem.at[1])
-    back_copy.start()
     sib = 1 - k
     for leaf in range(2):
         remote(
@@ -322,6 +325,9 @@
         c.start()
 
     total2 = nn(hat1[pl.ds(pl.multiple_of(x * PART, PART), PART)], up_v[1, rank_rows(x)])
+    back_v[...] = row_places(inverse_of(local), WIDE)
+    back_copy = pltpu.make_async_copy(back_v, back_s, place_sem.at[1])
+    back_copy.start()
     loads[2].wait()
     for i in range(B_NEAR):
         near_chunk(i)

time: 33.9 us -> 33.7 us (level)
  no operation moved by 1% of the time
where the time goes in v5:
time: 33.7 us; the launch traced here: 33.6 us
  Pallas kernels  32.9 us (98%)
  between operations  0.66 us (2%)
    pallas_call x1, Pallas kernels, on_device(): pl.pallas_call(tree_kernel, out_shape=(pltpu.VMEM((2 * FLAT, 128), F32),...  30.5 us
    pallas_call x1, Pallas kernels, on_device(): pl.pallas_call(leaf_kernel, out_shape=jax.ShapeDtypeStruct((FLAT, 128), F...  2.4 us

profile of v5, /device:TPU:1, one launch (start us, length us, event | category | flops | bytes accessed | tf_op | source)
XLA Modules:
  0.0 33.6 jit_solution(12862001415540411921)
XLA Ops:
  0.7 30.5 %tree.1 = (f32[16384,128]{1,0:T(8,128)S(1)}, bf16[2048,512]{1,0:T(8,128)(2,1)S(1)}, bf16[512,512]{1,0:T(8,128)(2,1)S(1)}, f32[8192,128]{1,0:T(8,128)S(1)}) custom-call(s32[16,128]{1,0:T(8,128)} %bitcast.12, f32[8192,128]{1,0:T(8,128)} %bitcast.11, bf16[2,1024,1024]{2,1,0:T(8,128)(2,1)} %near.1, bf16[2,1024,256]{2,1,0:T(8,128)(2,1)} %basis_in.1, ...), custom_call_target="tpu_custom_call" | custom-call | tf_op jit(solution)/shard_map/tree/pallas_call | solution.py:491
  31.2 2.4 %leaves.1 = f32[8192,128]{1,0:T(8,128)} custom-call(f32[1]{0:T(128)S(6)} %copy.11.ridge, f32[16384,128]{1,0:T(8,128)S(1)} %get-tuple-element.9.turned, bf16[2048,512]{1,0:T(8,128)(2,1)S(1)} %get-tuple-element.10.turned_basis, bf16[512,512]{1,0:T(8,128)(2,1)S(1)} %get-tuple-element.11.low0, f32[8192,128]{1,0:T(8,128)S(1)} %get-tuple-element.12.points), custom_call_target="tpu_custom_call" | custom-call | tf_op jit(solution)/shard_map/leaves/pallas_call | solution.py:564

commit v6 on v5

--- a/solution.py
+++ b/solution.py
@@ -335,7 +335,7 @@
     for h in (0, 1):
         rows = slice(h * BITE, (h + 1) * BITE)
         part = total2[rows]
-        for j in (1, 3, 2):
+        for j in (3, 1, 2):
             s = before(x, j)
             b_copies[j][h].wait_recv()
             part += nn(all1[s, rows], up_v[1, rank_rows(s)])
@@ -357,7 +357,7 @@
     for h in (0, 1):
         rows = slice(h * BITE, (h + 1) * BITE)
         part = total3[rows]
-        for j in (1, 3, 2):
+        for j in (3, 1, 2):
             s = before(gy, j)
             c_copies[j][h].wait_recv()
             part += nn(all2[s, rows], up_v[2, rank_rows(s)])
@@ -379,6 +379,8 @@
             + nt(sib0[1], lc_v[leaf, 2 - k])
         )
     turn(C_TURN, D_TURN)
+    for c in a_copies + bites(b_copies):
+        c.wait_send()
     loads[7].wait()
 
     e_copies = [None] + [
@@ -397,7 +399,7 @@
     for h in (0, 1):
         rows = slice(h * BITE, (h + 1) * BITE)
         far3 = jnp.zeros((BITE, RANK), F32)
-        for j in (1, 3, 2):
+        for j in (3, 1, 2):
             s = before(gx, j)
             d_copies[j][h].wait_recv()
             far3 += nt(all3[s, rows], nc_v[2, skip(s, gx)])
@@ -412,6 +414,8 @@
     far1[...] = total
     turn(C_TURN + D_TURN, GROUPS - C_TURN - D_TURN)
     turned_to_bf16(0, GROUPS)
+    for c in b2_copies[1:] + bites(c_copies):
+        c.wait_send()
     loads[6].wait()
     f_copies = []
 
@@ -440,16 +444,13 @@
             low0[rows, leaf * RANK : (leaf + 1) * RANK] = value.astype(BF16)
 
     leaf_down(mine)
+    for c in bites(d_copies) + bites(e_copies) + f_copies[:-1]:
+        c.wait_send()
     for n, (m, first, count) in enumerate(blocks):
         rows = pl.ds(pl.multiple_of(half_rows(1 - k, m, first), BITE), count)
         remote(low1.at[rows], low1.at[rows], f_send.at[n], f_recv.at[n], twin).wait_recv()
     leaf_down(other)
-
-    for c in a_copies + b2_copies[1:] + f_copies:
-        c.wait_send()
-    for kind in (b_copies, c_copies, d_copies, e_copies):
-        for c in bites(kind):
-            c.wait_send()
+    f_copies[-1].wait_send()
 
 
 def leaf_kernel(ridge, turned, turned_basis, low0, points, out, out_v, out_sem):

time: 33.7 us -> 33.6 us (level)
  no operation moved by 1% of the time
where the time goes in v6:
time: 33.6 us; the launch traced here: 33.5 us
  Pallas kernels  32.9 us (98%)
  between operations  0.66 us (2%)
    pallas_call x1, Pallas kernels, on_device(): pl.pallas_call(tree_kernel, out_shape=(pltpu.VMEM((2 * FLAT, 128), F32),...  30.5 us
    pallas_call x1, Pallas kernels, on_device(): pl.pallas_call(leaf_kernel, out_shape=jax.ShapeDtypeStruct((FLAT, 128), F...  2.4 us

profile of v6, /device:TPU:1, one launch (start us, length us, event | category | flops | bytes accessed | tf_op | source)
XLA Modules:
  0.0 33.5 jit_solution(286416267661348896)
XLA Ops:
  0.7 30.5 %tree.1 = (f32[16384,128]{1,0:T(8,128)S(1)}, bf16[2048,512]{1,0:T(8,128)(2,1)S(1)}, bf16[512,512]{1,0:T(8,128)(2,1)S(1)}, f32[8192,128]{1,0:T(8,128)S(1)}) custom-call(s32[16,128]{1,0:T(8,128)} %bitcast.12, f32[8192,128]{1,0:T(8,128)} %bitcast.11, bf16[2,1024,1024]{2,1,0:T(8,128)(2,1)} %near.1, bf16[2,1024,256]{2,1,0:T(8,128)(2,1)} %basis_in.1, ...), custom_call_target="tpu_custom_call" | custom-call | tf_op jit(solution)/shard_map/tree/pallas_call | solution.py:492
  31.1 2.4 %leaves.1 = f32[8192,128]{1,0:T(8,128)} custom-call(f32[1]{0:T(128)S(6)} %copy.11.ridge, f32[16384,128]{1,0:T(8,128)S(1)} %get-tuple-element.9.turned, bf16[2048,512]{1,0:T(8,128)(2,1)S(1)} %get-tuple-element.10.turned_basis, bf16[512,512]{1,0:T(8,128)(2,1)S(1)} %get-tuple-element.11.low0, f32[8192,128]{1,0:T(8,128)S(1)} %get-tuple-element.12.points), custom_call_target="tpu_custom_call" | custom-call | tf_op jit(solution)/shard_map/leaves/pallas_call | solution.py:565

commit v7 on v6

--- a/solution.py
+++ b/solution.py
@@ -230,7 +230,6 @@
     to_bf16(k)
     leaf_up(0, mine)
     leaf_up(1, mine)
-    a_copies[2].start()
 
     def near_chunk(i):
         leaf, q = i // 4, i % 4
@@ -323,6 +322,7 @@
         )
     for c in bites(b_copies):
         c.start()
+    a_copies[2].start()
 
     total2 = nn(hat1[pl.ds(pl.multiple_of(x * PART, PART), PART)], up_v[1, rank_rows(x)])
     back_v[...] = row_places(inverse_of(local), WIDE)
@@ -431,7 +431,7 @@
         f_copies.append(remote(low1.at[rows], low1.at[rows], f_send.at[n], f_recv.at[n], twin))
         f_copies[-1].start()
 
-    blocks = [(0, 0, PART)] + [(m, h * BITE, BITE) for h in (0, 1) for m in (3, 1, 2)]
+    blocks = [(0, 0, PART)] + [(m, h * BITE, BITE) for h in (0, 1) for m in (1, 3, 2)]
     for m, first, count in blocks:
         if m:
             e_copies[4 - m][first // BITE].wait_recv()

time: 33.6 us -> 33.6 us (level)
  no operation moved by 1% of the time
where the time goes in v7:
time: 33.6 us; the launch traced here: 33.5 us
  Pallas kernels  32.9 us (98%)
  between operations  0.66 us (2%)
    pallas_call x1, Pallas kernels, on_device(): pl.pallas_call(tree_kernel, out_shape=(pltpu.VMEM((2 * FLAT, 128), F32),...  30.5 us
    pallas_call x1, Pallas kernels, on_device(): pl.pallas_call(leaf_kernel, out_shape=jax.ShapeDtypeStruct((FLAT, 128), F...  2.4 us

profile of v7, /device:TPU:1, one launch (start us, length us, event | category | flops | bytes accessed | tf_op | source)
XLA Modules:
  0.0 33.5 jit_solution(11664771348763134068)
XLA Ops:
  0.7 30.5 %tree.1 = (f32[16384,128]{1,0:T(8,128)S(1)}, bf16[2048,512]{1,0:T(8,128)(2,1)S(1)}, bf16[512,512]{1,0:T(8,128)(2,1)S(1)}, f32[8192,128]{1,0:T(8,128)S(1)}) custom-call(s32[16,128]{1,0:T(8,128)} %bitcast.12, f32[8192,128]{1,0:T(8,128)} %bitcast.11, bf16[2,1024,1024]{2,1,0:T(8,128)(2,1)} %near.1, bf16[2,1024,256]{2,1,0:T(8,128)(2,1)} %basis_in.1, ...), custom_call_target="tpu_custom_call" | custom-call | tf_op jit(solution)/shard_map/tree/pallas_call | solution.py:492
  31.1 2.4 %leaves.1 = f32[8192,128]{1,0:T(8,128)} custom-call(f32[1]{0:T(128)S(6)} %copy.11.ridge, f32[16384,128]{1,0:T(8,128)S(1)} %get-tuple-element.9.turned, bf16[2048,512]{1,0:T(8,128)(2,1)S(1)} %get-tuple-element.10.turned_basis, bf16[512,512]{1,0:T(8,128)(2,1)S(1)} %get-tuple-element.11.low0, f32[8192,128]{1,0:T(8,128)S(1)} %get-tuple-element.12.points), custom_call_target="tpu_custom_call" | custom-call | tf_op jit(solution)/shard_map/leaves/pallas_call | solution.py:565
